TPU v7x, 512 devices: a whole 4x8x8 slice. The times are simulated.
512 devices in a mesh: resp: 32 (over y, z_hi), head: 16 (over z_lo, x, core).
Axes of the slice: x: 4, y: 8, z: 8 (z_hi: 4, z_lo: 2; z = z_hi * 2 + z_lo), core: 2. Of those that a mesh axis runs over, the one named last changes fastest.
Arguments:
- queries: bfloat16 [3072, 8192], P('resp', 'head'), may hold values from -5 to 5
- response_key_value: bfloat16 [3072, 2048], P('resp', 'head'), may hold values from -5 to 5
- prompt_key_value: bfloat16 [1024, 2048], P('resp', 'head'), may hold values from -5 to 5
- output_cotangent: bfloat16 [3072, 8192], P('resp', 'head'), may hold values from -5 to 5
- lengths: int32 [16], replicated, may hold values from 1 to 512, 3072 in all
Outputs:
- attended: bfloat16 [3072, 8192], P('resp', 'head')
- query_gradient: bfloat16 [3072, 8192], P('resp', 'head')
- response_key_value_gradient: bfloat16 [3072, 2048], P('resp', 'head')
- prompt_key_value_gradient: bfloat16 [1024, 2048], P('resp', 'head')
Inputs may be any that keep to these rules, and one draw needn't show every extreme that they name: The lengths sum to 3072, and the largest equals 512.
All inputs are finite; a program needn't handle non-finite values.
Results may differ from a plain program's by a relative error of at most 0.028.
Values may be sent and summed in bfloat16 or wider, within the bound.
A program may use at most 64 MiB of HBM per device.

v0:
```python
import math

import jax
import jax.numpy as jnp
from jax import lax
from jax.sharding import PartitionSpec as P

MAXLEN = 512


def partner(block, axis, bit):
    count = lax.axis_size(axis)
    route = []
    for low in range(count):
        high = low | 1 << bit
        if high != low and high < count:
            route += [(low, high), (high, low)]
    return lax.ppermute(block, axis, route)


def from_behind(x, axis, by):
    count = lax.axis_size(axis)
    pairs = [(i, i + by) for i in range(count) if 0 <= i + by < count]
    return lax.ppermute(x, axis, pairs)


def row_starts(lengths, row_ids):
    bounds = jnp.cumsum(lengths)
    before = (bounds[None, :] <= row_ids[:, None]).astype(jnp.int32)
    return jnp.sum(before * lengths[None, :], axis=1)


def split_kind(first, second, keys_side):
    owned = jnp.where(keys_side, first, second)
    others = jnp.where(keys_side, second, first)
    return (owned, others)


def shards(queries, response_key_value, prompt_key_value, output_cotangent, lengths):
    row_count = queries.shape[0]
    head_width = response_key_value.shape[1]
    head_count = queries.shape[1] // head_width
    prompt_local = prompt_key_value.shape[0]
    prompt_total = prompt_local * lax.axis_size("resp")
    reach_devices = (MAXLEN + row_count - 2) // row_count
    window_rows = (reach_devices + 1) * row_count
    logit_scale_factor = 1.0 / math.sqrt(head_width)
    keys_side = lax.axis_index("head") % 2 == 0
    own_rows = jnp.concatenate([prompt_key_value, response_key_value], axis=0)
    partner_rows = partner(own_rows, "head", 0)
    key_rows, value_rows = split_kind(own_rows, partner_rows, keys_side)
    local_full = jnp.concatenate([key_rows, value_rows], axis=1)
    prompt_full = local_full[:prompt_local]
    resp_full = local_full[prompt_local:]
    earlier = []
    for offset in range(reach_devices, 0, -1):
        earlier.append(from_behind(resp_full, "resp", offset))
    window = jnp.concatenate(earlier + [resp_full], axis=0)
    span_key_rows = window[:, :head_width]
    span_value_rows = window[:, head_width:]
    resp_index = lax.axis_index("resp")
    row_ids = resp_index * row_count + jnp.arange(row_count, dtype=jnp.int32)
    key_ids = (resp_index - reach_devices) * row_count + jnp.arange(window_rows, dtype=jnp.int32)
    starts = row_starts(lengths, row_ids)
    allowed = (key_ids[None, :] >= starts[:, None]) & (key_ids[None, :] <= row_ids[:, None])
    head_queries = jnp.transpose(queries.reshape(row_count, head_count, head_width), (1, 0, 2))
    head_grads = jnp.transpose(
        output_cotangent.reshape(row_count, head_count, head_width), (1, 0, 2)
    )

    def window_scores(query_head):
        scores = (
            jnp.einsum("rd,kd->rk", query_head, span_key_rows, preferred_element_type=jnp.float32)
            * logit_scale_factor
        )
        return jnp.where(allowed, scores, -jnp.inf)

    def window_stats(query_head):
        scores = window_scores(query_head)
        highest = jnp.max(scores, axis=1)
        totals = jnp.sum(jnp.exp(scores - highest[:, None]), axis=1)
        return (highest, totals)

    stats_start = lax.map(window_stats, head_queries)

    def stats_piece(carried, portion):
        highest, totals = carried
        scores = (
            jnp.einsum(
                "hrd,kd->hrk",
                head_queries,
                portion[:, :head_width],
                preferred_element_type=jnp.float32,
            )
            * logit_scale_factor
        )
        new_highest = jnp.maximum(highest, jnp.max(scores, axis=2))
        totals = totals * jnp.exp(highest - new_highest) + jnp.sum(
            jnp.exp(scores - new_highest[:, :, None]), axis=2
        )
        return (new_highest, totals)

    key_block = math.gcd(prompt_total, 512)
    block_total = prompt_total // key_block
    gathered = lax.all_gather(prompt_full, "resp", axis=0, tiled=True)

    def stats_block(block_index, carried):
        portion = lax.dynamic_slice_in_dim(gathered, block_index * key_block, key_block, 0)
        return stats_piece(carried, portion)

    highest, totals = lax.fori_loop(0, block_total, stats_block, stats_start)
    logsum = highest + jnp.log(totals)

    def window_output(head_inputs):
        query_head, logsum_head = head_inputs
        weights = jnp.exp(window_scores(query_head) - logsum_head[:, None]).astype(jnp.bfloat16)
        return jnp.dot(weights, span_value_rows, preferred_element_type=jnp.float32)

    output_start = lax.map(window_output, (head_queries, logsum))

    def output_piece(accumulated, portion):
        scores = (
            jnp.einsum(
                "hrd,kd->hrk",
                head_queries,
                portion[:, :head_width],
                preferred_element_type=jnp.float32,
            )
            * logit_scale_factor
        )
        weights = jnp.exp(scores - logsum[:, :, None]).astype(jnp.bfloat16)
        return accumulated + jnp.einsum(
            "hrk,kd->hrd", weights, portion[:, head_width:], preferred_element_type=jnp.float32
        )

    def output_block(block_index, carried):
        portion = lax.dynamic_slice_in_dim(gathered, block_index * key_block, key_block, 0)
        return output_piece(carried, portion)

    accumulated = lax.fori_loop(0, block_total, output_block, output_start)
    attention_output = accumulated.astype(jnp.bfloat16)
    delta = jnp.einsum(
        "hrd,hrd->hr", head_grads, attention_output, preferred_element_type=jnp.float32
    )

    def backward_piece(carried, portion, first_row):
        query_acc, key_full, value_full = carried
        piece_keys = portion[:, :head_width]
        piece_values = portion[:, head_width:]
        scores = (
            jnp.einsum("hrd,kd->hrk", head_queries, piece_keys, preferred_element_type=jnp.float32)
            * logit_scale_factor
        )
        weights = jnp.exp(scores - logsum[:, :, None])
        dweight = jnp.einsum(
            "hrd,kd->hrk", head_grads, piece_values, preferred_element_type=jnp.float32
        )
        dscore = (weights * (dweight - delta[:, :, None])).astype(jnp.bfloat16)
        query_acc = query_acc + jnp.einsum(
            "hrk,kd->hrd", dscore, piece_keys, preferred_element_type=jnp.float32
        )
        key_grad = (
            jnp.einsum("hrk,hrd->kd", dscore, head_queries, preferred_element_type=jnp.float32)
            * logit_scale_factor
        )
        value_grad = jnp.einsum(
            "hrk,hrd->kd",
            weights.astype(jnp.bfloat16),
            head_grads,
            preferred_element_type=jnp.float32,
        )
        key_full = lax.dynamic_update_slice_in_dim(key_full, key_grad, first_row, 0)
        value_full = lax.dynamic_update_slice_in_dim(value_full, value_grad, first_row, 0)
        return (query_acc, key_full, value_full)

    begin_grads = (
        jnp.zeros_like(accumulated),
        jnp.zeros((prompt_total, head_width), jnp.float32),
        jnp.zeros((prompt_total, head_width), jnp.float32),
    )

    def backward_block(block_index, carried):
        portion = lax.dynamic_slice_in_dim(gathered, block_index * key_block, key_block, 0)
        return backward_piece(carried, portion, block_index * key_block)

    query_prompt, key_full, value_full = lax.fori_loop(0, block_total, backward_block, begin_grads)

    def window_backward(carried, head_inputs):
        key_span_rows, value_span_rows = carried
        query_head, grad_head, logsum_head, delta_head = head_inputs
        weights = jnp.exp(window_scores(query_head) - logsum_head[:, None])
        dweight = jnp.einsum(
            "rd,kd->rk", grad_head, span_value_rows, preferred_element_type=jnp.float32
        )
        dscore = (weights * (dweight - delta_head[:, None])).astype(jnp.bfloat16)
        query_window = jnp.dot(dscore, span_key_rows, preferred_element_type=jnp.float32)
        key_span_rows = (
            key_span_rows
            + jnp.einsum("rk,rd->kd", dscore, query_head, preferred_element_type=jnp.float32)
            * logit_scale_factor
        )
        value_span_rows = value_span_rows + jnp.einsum(
            "rk,rd->kd", weights.astype(jnp.bfloat16), grad_head, preferred_element_type=jnp.float32
        )
        return ((key_span_rows, value_span_rows), query_window)

    window_start = (
        jnp.zeros((window_rows, head_width), jnp.float32),
        jnp.zeros((window_rows, head_width), jnp.float32),
    )
    window_sums, query_window = lax.scan(
        window_backward, window_start, (head_queries, head_grads, logsum, delta)
    )
    query_total = ((query_prompt + query_window) * logit_scale_factor).astype(jnp.bfloat16)
    window_grads = jnp.concatenate([window_sums[0], window_sums[1]], axis=1)
    response_gradient_parts = window_grads[reach_devices * row_count :]
    for offset in range(1, reach_devices + 1):
        portion = window_grads[
            (reach_devices - offset) * row_count : (reach_devices - offset + 1) * row_count
        ]
        response_gradient_parts = response_gradient_parts + from_behind(
            portion.astype(jnp.bfloat16), "resp", -offset
        ).astype(portion.dtype)
    resp_owned, resp_others = split_kind(
        response_gradient_parts[:, :head_width], response_gradient_parts[:, head_width:], keys_side
    )
    key_reduced, value_reduced = (
        lax.psum_scatter(key_full, "resp", scatter_dimension=0, tiled=True),
        lax.psum_scatter(value_full, "resp", scatter_dimension=0, tiled=True),
    )
    prompt_owned, prompt_others = split_kind(key_reduced, value_reduced, keys_side)
    sending = jnp.concatenate([prompt_others, resp_others], axis=0)
    arriving = partner(sending.astype(jnp.bfloat16), "head", 0).astype(sending.dtype)
    summed = jnp.concatenate([prompt_owned, resp_owned], axis=0) + arriving
    prompt_result = summed[:prompt_local]
    resp_result = summed[prompt_local:]
    attended = jnp.transpose(attention_output, (1, 0, 2)).reshape(
        row_count, head_count * head_width
    )
    query_gradient = jnp.transpose(query_total, (1, 0, 2)).reshape(
        row_count, head_count * head_width
    )
    return (
        attended,
        query_gradient,
        resp_result.astype(jnp.bfloat16),
        prompt_result.astype(jnp.bfloat16),
    )


def solution(mesh):
    return jax.shard_map(
        shards,
        mesh=mesh,
        in_specs=(P("resp", "head"), P("resp", "head"), P("resp", "head"), P("resp", "head"), P()),
        out_specs=(P("resp", "head"), P("resp", "head"), P("resp", "head"), P("resp", "head")),
        check_vma=False,
    )
```

profile of v0, /device:TPU:1, one launch (start us, length us, event | category | flops | bytes accessed | tf_op | source)
XLA Modules:
  0.0 614.4 jit_solution(5211444578935842848)
XLA Ops:
  8.7 8.8 %collective-permute-start = (bf16[128,128]{1,0:T(8,128)(2,1)S(1)}, bf16[128,128]{1,0:T(8,128)(2,1)S(1)}, u32[]{:S(2)}, u32[]{:S(2)}) collective-permute-start(bf16[128,128]{1,0:T(8,128)(2,1)S(1)} %constant_dynamic-update-slice_fusion), channel_id=1, source_target_pairs={{0,1},{1,0},{2,3},{3,2},{4,5},{5,4},{6,7},{7,6},{8,9},{9,8},{10,11... | collective-permute-start | bytes 98312 | tf_op jit(solution)/shard_map/ppermute | solution.py:18
  20.2 6.3 %collective-permute-start.1 = (bf16[96,256]{1,0:T(8,128)(2,1)S(1)}, bf16[96,256]{1,0:T(8,128)(2,1)S(1)}, u32[]{:S(2)}, u32[]{:S(2)}) collective-permute-start(bf16[96,256]{1,0:T(8,128)(2,1)S(1)} %fusion.89), channel_id=1, source_target_pairs={{0,96},{16,112},{32,128},{48,144},{64,160},{80,176},{96,192},{112,... | collective-permute-start | bytes 147464 | tf_op jit(solution)/shard_map/ppermute | solution.py:24
  26.5 5.0 collective-permute-start.2
  31.5 3.2 collective-permute-start.3
  34.7 5.6 collective-permute-start.4
  40.3 1.5 collective-permute-start.5
  41.9 67.4 %all_gather.3 = bf16[1024,256]{1,0:T(8,128)(2,1)S(1)} all-gather(bf16[32,256]{1,0:T(8,128)(2,1)S(1)} %pad_maximum_fusion.1), channel_id=1, replica_groups=mesh['resp'=32,'head'=16] {'resp'}, dimensions={0}, use_global_device_ids=true | all-gather | bytes 540672 | tf_op jit(solution)/shard_map/all_gather | solution.py:105
  109.2 2.4 collective-permute-start.6
  112.9 2.4 while.87
  115.3 1.4 while.85
  116.8 1.6 while.88
  121.3 7.0 %while.89 = (s32[]{:T(128)}, f32[4,96,128]{2,1,0:T(8,128)S(1)}, f32[1024,128]{1,0:T(8,128)}, f32[1024,128]{1,0:T(8,128)}, bf16[1024,256]{1,0:T(8,128)(2,1)S(1)},...) while((s32[]{:T(128)}, f32[4,96,128]{2,1,0:T(8,128)S(1)}, ...), condition=%wide.region_15.16_spmd.clone, body=%wide.region_14.15_spmd.clone.sunk | while | flops 253001728 | bytes 13635929 | solution.py:186
  128.4 5.1 while.90
  133.7 1.3 collective-permute-start.12
  135.0 1.3 collective-permute-start.11
  136.3 1.3 collective-permute-start.10
  137.6 1.3 collective-permute-start.9
  138.9 1.3 collective-permute-start.8
  140.2 3.1 collective-permute-done.12
  145.3 2.3 collective-permute-done.8
  147.6 2.1 collective-permute-done.7
  149.8 219.1 %reduce-scatter.3.cloned.1.call-done = f32[32,128]{1,0:T(8,128)} async-done(((f32[1024,128]{1,0:T(8,128)}), f32[32,128]{1,0:T(8,128)}) %reduce-scatter.3.cloned.1.call-update) | async-done | bytes 16400 | tf_op jit(solution)/shard_map/reduce_scatter | solution.py:228
  368.9 228.7 %reduce-scatter.5.cloned.1.call-done = f32[32,128]{1,0:T(8,128)} async-done(((f32[1024,128]{1,0:T(8,128)}), f32[32,128]{1,0:T(8,128)}) %reduce-scatter.5.cloned.1.call-update) | async-done | bytes 16400 | tf_op jit(solution)/shard_map/reduce_scatter | solution.py:229
  598.3 7.2 %collective-permute-start.13 = (bf16[128,128]{1,0:T(8,128)(2,1)S(1)}, bf16[128,128]{1,0:T(8,128)(2,1)S(1)}, u32[]{:S(2)}, u32[]{:S(2)}) collective-permute-start(bf16[128,128]{1,0:T(8,128)(2,1)S(1)} %pad_maximum_fusion), channel_id=1, source_target_pairs={{0,1},{1,0},{2,3},{3,2},{4,5},{5,4},{6,7},{7,6},{8,9},{9,8},{10,11... | collective-permute-start | bytes 98312 | tf_op jit(solution)/shard_map/ppermute | solution.py:18
  (163 shorter events, 31.0 us)
Async XLA Ops:
  7.2 12.0 %copy-start.4 = (bf16[96,512]{1,0:T(8,128)(2,1)S(1)}, bf16[96,512]{1,0:T(8,128)(2,1)}, u32[]{:S(2)}) copy-start(bf16[96,512]{1,0:T(8,128)(2,1)} %param.17) | copy-start | bytes 294916
  7.2 361.7 %reduce-scatter.3.cloned.1.call-start = ((), (), s32[]{:S(2)}) async-start(), calls=%async_computation.2 | async-start | bytes 540672 | tf_op jit(solution)/shard_map/reduce_scatter | solution.py:228
  8.7 11.5 %collective-permute-start = (bf16[128,128]{1,0:T(8,128)(2,1)S(1)}, bf16[128,128]{1,0:T(8,128)(2,1)S(1)}, u32[]{:S(2)}, u32[]{:S(2)}) collective-permute-start(bf16[128,128]{1,0:T(8,128)(2,1)S(1)} %constant_dynamic-update-slice_fusion), channel_id=1, source_target_pairs={{0,1},{1,0},{2,3},{3,2},{4,5},{5,4},{6,7},{7,6},{8,9},{9,8},{10,11... | collective-permute-start | bytes 98312 | tf_op jit(solution)/shard_map/ppermute | solution.py:18
  19.2 0.9 copy-start.5
  20.2 89.0 %collective-permute-start.1 = (bf16[96,256]{1,0:T(8,128)(2,1)S(1)}, bf16[96,256]{1,0:T(8,128)(2,1)S(1)}, u32[]{:S(2)}, u32[]{:S(2)}) collective-permute-start(bf16[96,256]{1,0:T(8,128)(2,1)S(1)} %fusion.89), channel_id=1, source_target_pairs={{0,96},{16,112},{32,128},{48,144},{64,160},{80,176},{96,192},{112,... | collective-permute-start | bytes 147464 | tf_op jit(solution)/shard_map/ppermute | solution.py:24
  26.5 85.2 %collective-permute-start.2 = (bf16[96,256]{1,0:T(8,128)(2,1)S(1)}, bf16[96,256]{1,0:T(8,128)(2,1)S(1)}, u32[]{:S(2)}, u32[]{:S(2)}) collective-permute-start(bf16[96,256]{1,0:T(8,128)(2,1)S(1)} %fusion.89), channel_id=1, source_target_pairs={{0,80},{16,96},{32,112},{48,128},{64,144},{80,160},{96,176},{112,1... | collective-permute-start | bytes 147464 | tf_op jit(solution)/shard_map/ppermute | solution.py:24
  31.5 80.2 %collective-permute-start.3 = (bf16[96,256]{1,0:T(8,128)(2,1)S(1)}, bf16[96,256]{1,0:T(8,128)(2,1)S(1)}, u32[]{:S(2)}, u32[]{:S(2)}) collective-permute-start(bf16[96,256]{1,0:T(8,128)(2,1)S(1)} %fusion.89), channel_id=1, source_target_pairs={{0,64},{16,80},{32,96},{48,112},{64,128},{80,144},{96,160},{112,17... | collective-permute-start | bytes 147464 | tf_op jit(solution)/shard_map/ppermute | solution.py:24
  34.7 77.0 %collective-permute-start.4 = (bf16[96,256]{1,0:T(8,128)(2,1)S(1)}, bf16[96,256]{1,0:T(8,128)(2,1)S(1)}, u32[]{:S(2)}, u32[]{:S(2)}) collective-permute-start(bf16[96,256]{1,0:T(8,128)(2,1)S(1)} %fusion.89), channel_id=1, source_target_pairs={{0,48},{16,64},{32,80},{48,96},{64,112},{80,128},{96,144},{112,160... | collective-permute-start | bytes 147464 | tf_op jit(solution)/shard_map/ppermute | solution.py:24
  40.3 71.4 %collective-permute-start.5 = (bf16[96,256]{1,0:T(8,128)(2,1)S(1)}, bf16[96,256]{1,0:T(8,128)(2,1)S(1)}, u32[]{:S(2)}, u32[]{:S(2)}) collective-permute-start(bf16[96,256]{1,0:T(8,128)(2,1)S(1)} %fusion.89), channel_id=1, source_target_pairs={{0,32},{16,48},{32,64},{48,80},{64,96},{80,112},{96,128},{112,144}... | collective-permute-start | bytes 147464 | tf_op jit(solution)/shard_map/ppermute | solution.py:24
  109.2 3.6 collective-permute-start.6
  121.9 1.0 copy-start
  122.2 1.1 copy-start.2
  125.4 1.0 copy-start
  125.7 1.1 copy-start.2
  128.3 469.2 %reduce-scatter.5.cloned.1.call-start = ((), (), s32[]{:S(2)}) async-start(), calls=%async_computation.3 | async-start | bytes 540672 | tf_op jit(solution)/shard_map/reduce_scatter | solution.py:229
  133.7 9.6 %collective-permute-start.12 = (bf16[96,256]{1,0:T(8,128)(2,1)S(1)}, bf16[96,256]{1,0:T(8,128)(2,1)S(1)}, u32[]{:S(2)}, u32[]{:S(2)}) collective-permute-start(bf16[96,256]{1,0:T(8,128)(2,1)S(1)} %get-tuple-element.814), channel_id=1, source_target_pairs={{96,0},{112,16},{128,32},{144,48},{160,64},{176,80},{192,96},{208,... | collective-permute-start | bytes 147464 | tf_op jit(solution)/shard_map/ppermute | solution.py:24
  135.0 10.3 %collective-permute-start.11 = (bf16[96,256]{1,0:T(8,128)(2,1)S(1)}, bf16[96,256]{1,0:T(8,128)(2,1)S(1)}, u32[]{:S(2)}, u32[]{:S(2)}) collective-permute-start(bf16[96,256]{1,0:T(8,128)(2,1)S(1)} %get-tuple-element.815), channel_id=1, source_target_pairs={{80,0},{96,16},{112,32},{128,48},{144,64},{160,80},{176,96},{192,1... | collective-permute-start | bytes 147464 | tf_op jit(solution)/shard_map/ppermute | solution.py:24
  136.3 9.0 %collective-permute-start.10 = (bf16[96,256]{1,0:T(8,128)(2,1)S(1)}, bf16[96,256]{1,0:T(8,128)(2,1)S(1)}, u32[]{:S(2)}, u32[]{:S(2)}) collective-permute-start(bf16[96,256]{1,0:T(8,128)(2,1)S(1)} %get-tuple-element.816), channel_id=1, source_target_pairs={{64,0},{80,16},{96,32},{112,48},{128,64},{144,80},{160,96},{176,11... | collective-permute-start | bytes 147464 | tf_op jit(solution)/shard_map/ppermute | solution.py:24
  137.6 7.8 %collective-permute-start.9 = (bf16[96,256]{1,0:T(8,128)(2,1)S(1)}, bf16[96,256]{1,0:T(8,128)(2,1)S(1)}, u32[]{:S(2)}, u32[]{:S(2)}) collective-permute-start(bf16[96,256]{1,0:T(8,128)(2,1)S(1)} %get-tuple-element.817), channel_id=1, source_target_pairs={{48,0},{64,16},{80,32},{96,48},{112,64},{128,80},{144,96},{160,112... | collective-permute-start | bytes 147464 | tf_op jit(solution)/shard_map/ppermute | solution.py:24
  138.9 8.7 %collective-permute-start.8 = (bf16[96,256]{1,0:T(8,128)(2,1)S(1)}, bf16[96,256]{1,0:T(8,128)(2,1)S(1)}, u32[]{:S(2)}, u32[]{:S(2)}) collective-permute-start(bf16[96,256]{1,0:T(8,128)(2,1)S(1)} %get-tuple-element.818), channel_id=1, source_target_pairs={{32,0},{48,16},{64,32},{80,48},{96,64},{112,80},{128,96},{144,112}... | collective-permute-start | bytes 147464 | tf_op jit(solution)/shard_map/ppermute | solution.py:24
  143.3 6.4 %collective-permute-start.7 = (bf16[96,256]{1,0:T(8,128)(2,1)S(1)}, bf16[96,256]{1,0:T(8,128)(2,1)S(1)}, u32[]{:S(2)}, u32[]{:S(2)}) collective-permute-start(bf16[96,256]{1,0:T(8,128)(2,1)S(1)} %get-tuple-element.813), channel_id=1, source_target_pairs={{16,0},{32,16},{48,32},{64,48},{80,64},{96,80},{112,96},{128,112},... | collective-permute-start | bytes 147464 | tf_op jit(solution)/shard_map/ppermute | solution.py:24
  598.3 7.2 %copy-start.6 = (f32[32,128]{1,0:T(8,128)S(1)}, f32[32,128]{1,0:T(8,128)}, u32[]{:S(2)}) copy-start(f32[32,128]{1,0:T(8,128)} %reduce-scatter.3.cloned.1.call-done) | copy-start | bytes 49156
  598.3 7.2 %copy-start.7 = (f32[32,128]{1,0:T(8,128)S(1)}, f32[32,128]{1,0:T(8,128)}, u32[]{:S(2)}) copy-start(f32[32,128]{1,0:T(8,128)} %reduce-scatter.5.cloned.1.call-done) | copy-start | bytes 49156
  598.3 8.0 %collective-permute-start.13 = (bf16[128,128]{1,0:T(8,128)(2,1)S(1)}, bf16[128,128]{1,0:T(8,128)(2,1)S(1)}, u32[]{:S(2)}, u32[]{:S(2)}) collective-permute-start(bf16[128,128]{1,0:T(8,128)(2,1)S(1)} %pad_maximum_fusion), channel_id=1, source_target_pairs={{0,1},{1,0},{2,3},{3,2},{4,5},{5,4},{6,7},{7,6},{8,9},{9,8},{10,11... | collective-permute-start | bytes 98312 | tf_op jit(solution)/shard_map/ppermute | solution.py:18
  (5 other events, 3.8 us)
Sparse Core Ops, SparseCore 0:
  128.5 240.3 reduce-scatter.2
  374.0 223.5 reduce-scatter.4
where the time goes:
time: 615 us; the launch traced here: 614 us
  waiting for transfers between devices  457 us (74%)
  blocking collectives  67.4 us (11%)
  starting transfers between devices  47.8 us (8%)
  between operations  14.6 us (2%)
  matrix products  12 us (2%)
  local copies, waits for them, and re-layouts  11.3 us (2%)
    reduce_scatter x1, waiting for transfers between devices, shards(): lax.psum_scatter(value_full, 'resp', scatter_dimension=0, tiled=True)  229 us
    reduce_scatter x1, waiting for transfers between devices, shards(): lax.psum_scatter(key_full, 'resp', scatter_dimension=0, tiled=True)  219 us
    all_gather x1, blocking collectives, shards(): gathered = lax.all_gather(prompt_full, 'resp', axis=0, tiled=True)  67.4 us
    ppermute x12, starting transfers between devices, from_behind(): return lax.ppermute(x, axis, pairs)  31.8 us
    ppermute x2, starting transfers between devices, partner(): return lax.ppermute(block, axis, route)  16 us
  transfers between devices with their start and end apart: 16, of which 7 were waited for; matrix products, arithmetic and copies ran while one was open for 1% of the time, Pallas kernels for 0%

commit v1 on v0

v1 whole, which is shorter than its diff:
```python
import functools
import math

import jax
import jax.numpy as jnp
from jax import lax
from jax.experimental import pallas as pl
from jax.experimental.pallas import tpu as pltpu
from jax.sharding import PartitionSpec as P

MAXLEN = 512
GROUP = 4
MESH = pl.DeviceIdType.MESH
F32 = jnp.float32
BF16 = jnp.bfloat16


def dot(a, b, ca, cb):
    return lax.dot_general(a, b, (((ca,), (cb,)), ((), ())), preferred_element_type=F32)


def wait_bytes(ref, sem):
    pltpu.make_async_copy(ref, ref, sem).wait()


def kernel(
    count,
    q_hbm, kv_hbm, pkv_hbm, do_hbm, len_ref,
    att_hbm, dq_hbm, dkv_hbm, dpkv_hbm,
    qs, dos, kvp, kvw, ebuf, dpbuf, mbuf, wbuf, dsbuf,
    gp, gpin, gpout, rs, gw, gwin, gwout, wr, os, dqs, dkvs, dpkvs,
    load_sem, kv_sem, p_send, p_recv, pf_send, pf_recv, w_send, w_recv, wf_send, wf_recv,
    gx_send, gx_recv, gwx_send, gwx_recv, rs_send, rs_recv, wr_send, wr_recv, out_sem,
):
    rows, width = q_hbm.shape
    d = kv_hbm.shape[1]
    heads = width // d
    cols = heads * rows
    plocal = pkv_hbm.shape[0]
    groups = count // GROUP
    chunk = GROUP * plocal
    reach = kvw.shape[1] // rows - 1
    scale = 1.0 / math.sqrt(d)
    to_log2 = scale * math.log2(math.e)

    me = lax.axis_index("resp")
    head = lax.axis_index("head")
    kind = lax.rem(head, 2)
    other = 1 - kind
    mate = {"head": head + 1 - 2 * kind}
    my_group = me // GROUP
    my_place = lax.rem(me, GROUP)

    def peer(by):
        return lax.rem(me + by + count, count)

    def remote(src, dst, send, recv, to):
        copy = pltpu.make_async_remote_copy(
            src_ref=src, dst_ref=dst, send_sem=send, recv_sem=recv, device_id=to, device_id_type=MESH
        )
        copy.start()

    def prompt_rows(index, size):
        return pl.ds(pl.multiple_of(index * size, size), size)

    own_p = prompt_rows(me, plocal)
    own_w = pl.ds(reach * rows, rows)
    kv_copy = pltpu.make_async_copy(kv_hbm, kvw.at[kind, own_w], kv_sem.at[0])
    pkv_copy = pltpu.make_async_copy(pkv_hbm, kvp.at[kind, own_p], kv_sem.at[1])
    kv_copy.start()
    pkv_copy.start()
    for h in range(heads):
        pltpu.make_async_copy(
            q_hbm.at[:, pl.ds(h * d, d)], qs.at[pl.ds(h * rows, rows)], load_sem.at[0]
        ).start()
        pltpu.make_async_copy(
            do_hbm.at[:, pl.ds(h * d, d)], dos.at[pl.ds(h * rows, rows)], load_sem.at[1]
        ).start()

    barrier = pltpu.get_barrier_semaphore()
    pl.semaphore_signal(barrier, inc=1, device_id=mate, device_id_type=MESH)
    for by in range(1, count):
        pl.semaphore_signal(barrier, inc=1, device_id={"resp": peer(by)}, device_id_type=MESH)
    pl.semaphore_wait(barrier, count)

    kv_copy.wait()
    pkv_copy.wait()
    remote(kvw.at[kind, own_w], kvw.at[kind, own_w], wf_send, wf_recv.at[reach], mate)
    for by in range(1, count):
        remote(
            kvp.at[kind, own_p], kvp.at[kind, own_p], p_send, p_recv.at[my_group],
            {"resp": peer(by)},
        )
    for off in range(1, reach + 1):
        slot = reach - off
        remote(
            kvw.at[kind, own_w], kvw.at[kind, pl.ds(slot * rows, rows)], w_send, w_recv.at[slot],
            {"resp": peer(off)},
        )

    lane = lax.broadcasted_iota(jnp.int32, (1, cols), 1)
    row_id = lane
    for h in range(1, heads):
        row_id = row_id - jnp.where(lane >= h * rows, rows, 0)
    row_id = row_id + me * rows
    start = jnp.zeros((1, cols), jnp.int32)
    bound = jnp.int32(0)
    for j in range(len_ref.shape[0]):
        length = len_ref[j]
        bound = bound + length
        start = start + jnp.where(bound <= row_id, length, 0)

    wait_bytes(qs, load_sem.at[0])
    wait_bytes(dos, load_sem.at[1])

    stats = [None, None, None]

    def forward(index, keys, values, base, size, off=None):
        s = dot(keys, qs[...], 1, 1) * to_log2
        if off is not None:
            key_id = lax.broadcasted_iota(jnp.int32, (size, cols), 0) + (me - off) * rows
            allowed = key_id >= start
            if off == 0:
                allowed = allowed & (key_id <= row_id)
            s = jnp.where(allowed, s, -jnp.inf)
        dp = dot(values, dos[...], 1, 1)
        high = jnp.max(s, axis=0, keepdims=True)
        if stats[0] is not None:
            high = jnp.maximum(high, stats[0])
        e = jnp.exp2(s - high)
        total = jnp.sum(e, axis=0, keepdims=True)
        weighted = jnp.sum(e * dp, axis=0, keepdims=True)
        if stats[0] is not None:
            shrink = jnp.exp2(stats[0] - high)
            total = total + stats[1] * shrink
            weighted = weighted + stats[2] * shrink
        stats[0], stats[1], stats[2] = high, total, weighted
        ebuf[base, :] = e
        dpbuf[base, :] = dp
        mbuf[index] = jnp.broadcast_to(high, (8, cols))

    total_p = groups * chunk

    def group_at(n):
        return lax.rem(my_group + n, groups)

    def w_rows(slot):
        return pl.ds(slot * rows, rows)

    def e_w_rows(slot):
        return pl.ds(total_p + slot * rows, rows)

    wait_bytes(kvw.at[other, own_w], wf_recv.at[reach])
    forward(groups + reach, kvw[0, own_w], kvw[1, own_w], e_w_rows(reach), rows, 0)

    order = sorted(range(groups), key=lambda n: min(n, groups - n))
    steps = [("p", n) for n in order] + [("w", s) for s in range(reach - 1, -1, -1)]

    def forward_step(step):
        what, n = step
        if what == "p":
            g = group_at(n)
            at = prompt_rows(g, chunk)
            wait_bytes(kvp.at[other, at], pf_recv.at[g])
            forward(g, kvp[0, at], kvp[1, at], at, chunk)
        else:
            wait_bytes(kvw.at[other, w_rows(n)], wf_recv.at[n])
            forward(groups + n, kvw[0, w_rows(n)], kvw[1, w_rows(n)], e_w_rows(n), rows, reach - n)

    before = None
    for step in steps:
        what, n = step
        if what == "p":
            g = group_at(n)
            at = prompt_rows(g, chunk)
            got = (GROUP - 1 if n == 0 else GROUP) * plocal
            wait_bytes(kvp.at[kind, pl.ds(0, got)], p_recv.at[g])
            remote(kvp.at[kind, at], kvp.at[kind, at], pf_send, pf_recv.at[g], mate)
        else:
            wait_bytes(kvw.at[kind, w_rows(n)], w_recv.at[n])
            remote(kvw.at[kind, w_rows(n)], kvw.at[kind, w_rows(n)], wf_send, wf_recv.at[n], mate)
        if before is not None:
            forward_step(before)
        before = step
    forward_step(before)

    high, total, weighted = stats
    inverse = 1.0 / total
    delta = weighted * inverse

    def backward(index, base):
        factor = jnp.exp2(mbuf[index][:1] - high) * inverse
        w = ebuf[base, :] * factor
        wb = w.astype(BF16)
        ds = (w * (dpbuf[base, :] - delta)).astype(BF16)
        wbuf[base, :] = wb
        dsbuf[base, :] = ds
        return dot(ds, qs[...], 1, 0) * scale, dot(wb, dos[...], 1, 0)

    def finish_prompt(n):
        g = group_at(n)
        at = prompt_rows(g, chunk)
        wait_bytes(gpin.at[at], gx_recv.at[g])
        gpout[at, :] = (gp[kind, at].astype(F32) + gpin[at, :].astype(F32)).astype(BF16)
        for k in range(1 if n == 0 else 0, GROUP):
            to = g * GROUP + lax.rem(my_place + k, GROUP)
            remote(
                gpout.at[prompt_rows(to, plocal)], rs.at[me], rs_send, rs_recv, {"resp": to}
            )
        if n == 0:
            rs[me] = gpout[own_p, :]

    def finish_window(s):
        wait_bytes(gwin.at[s], gwx_recv.at[s])
        both = gw[kind, s].astype(F32) + gwin[s].astype(F32)
        if s == reach:
            return both
        gwout[s] = both.astype(BF16)
        off = reach - s
        remote(gwout.at[s], wr.at[off - 1], wr_send, wr_recv.at[off - 1], {"resp": peer(-off)})
        return None

    def backward_step(step):
        what, n = step
        if what == "p":
            g = group_at(n)
            at = prompt_rows(g, chunk)
            dk, dv = backward(g, at)
            gp[0, at] = dk.astype(BF16)
            gp[1, at] = dv.astype(BF16)
            remote(gp.at[other, at], gpin.at[at], gx_send, gx_recv.at[g], mate)
        else:
            dk, dv = backward(groups + n, e_w_rows(n))
            gw[0, n] = dk.astype(BF16)
            gw[1, n] = dv.astype(BF16)
            remote(gw.at[other, n], gwin.at[n], gwx_send, gwx_recv.at[n], mate)

    def finish(step):
        return finish_prompt(step[1]) if step[0] == "p" else finish_window(step[1])

    back = [("w", s) for s in range(reach)] + [("p", n) for n in reversed(order)] + [("w", reach)]
    before = None
    for step in back:
        backward_step(step)
        if before is not None:
            finish(before)
        before = step

    values_p = kvp[1]
    values_w = kvw[1]
    p_part = pl.ds(0, total_p)
    w_part = pl.ds(total_p, (reach + 1) * rows)
    out_t = dot(values_p, wbuf[p_part, :], 0, 0) + dot(values_w, wbuf[w_part, :], 0, 0)
    os[...] = out_t.T.astype(BF16)
    own_grad = finish(before)
    for h in range(heads):
        pltpu.make_async_copy(
            os.at[pl.ds(h * rows, rows)], att_hbm.at[:, pl.ds(h * d, d)], out_sem.at[0]
        ).start()
    dq_t = dot(kvp[0], dsbuf[p_part, :], 0, 0) + dot(kvw[0], dsbuf[w_part, :], 0, 0)
    dqs[...] = (dq_t.T * scale).astype(BF16)
    for h in range(heads):
        pltpu.make_async_copy(
            dqs.at[pl.ds(h * rows, rows)], dq_hbm.at[:, pl.ds(h * d, d)], out_sem.at[1]
        ).start()

    for off in range(1, reach + 1):
        wait_bytes(wr.at[off - 1], wr_recv.at[off - 1])
        own_grad = own_grad + wr[off - 1].astype(F32)
    dkvs[...] = own_grad.astype(BF16)
    dkv_copy = pltpu.make_async_copy(dkvs, dkv_hbm, out_sem.at[2])
    dkv_copy.start()
    wait_bytes(rs.at[pl.ds(0, count - 1)], rs_recv)
    dpkvs[...] = jnp.sum(rs[...].astype(F32), axis=0).astype(BF16)
    dpkv_copy = pltpu.make_async_copy(dpkvs, dpkv_hbm, out_sem.at[3])
    dpkv_copy.start()

    wait_bytes(kvp.at[0, pl.ds(0, (count - 1) * plocal)], p_send)
    wait_bytes(kvp.at[0], pf_send)
    wait_bytes(kvw.at[0, pl.ds(0, reach * rows)], w_send)
    wait_bytes(kvw.at[0], wf_send)
    wait_bytes(gpin, gx_send)
    wait_bytes(gwin, gwx_send)
    wait_bytes(rs.at[pl.ds(0, count - 1)], rs_send)
    wait_bytes(wr, wr_send)
    wait_bytes(os, out_sem.at[0])
    wait_bytes(dqs, out_sem.at[1])
    dkv_copy.wait()
    dpkv_copy.wait()


def shards(queries, response_key_value, prompt_key_value, output_cotangent, lengths):
    rows, width = queries.shape
    d = response_key_value.shape[1]
    cols = width // d * rows
    plocal = prompt_key_value.shape[0]
    count = lax.axis_size("resp")
    total_p = plocal * count
    groups = count // GROUP
    reach = (MAXLEN + rows - 2) // rows
    keys = total_p + (reach + 1) * rows
    dma, anywhere = pltpu.SemaphoreType.DMA, pl.BlockSpec(memory_space=pl.ANY)
    return pl.pallas_call(
        functools.partial(kernel, count),
        out_shape=(
            jax.ShapeDtypeStruct(queries.shape, BF16),
            jax.ShapeDtypeStruct(queries.shape, BF16),
            jax.ShapeDtypeStruct(response_key_value.shape, BF16),
            jax.ShapeDtypeStruct(prompt_key_value.shape, BF16),
        ),
        in_specs=[anywhere] * 4 + [pl.BlockSpec(memory_space=pltpu.SMEM)],
        out_specs=(anywhere,) * 4,
        scratch_shapes=[
            pltpu.VMEM((cols, d), BF16),
            pltpu.VMEM((cols, d), BF16),
            pltpu.VMEM((2, total_p, d), BF16),
            pltpu.VMEM((2, (reach + 1) * rows, d), BF16),
            pltpu.VMEM((keys, cols), F32),
            pltpu.VMEM((keys, cols), F32),
            pltpu.VMEM((groups + reach + 1, 8, cols), F32),
            pltpu.VMEM((keys, cols), BF16),
            pltpu.VMEM((keys, cols), BF16),
            pltpu.VMEM((2, total_p, d), BF16),
            pltpu.VMEM((total_p, d), BF16),
            pltpu.VMEM((total_p, d), BF16),
            pltpu.VMEM((count, plocal, d), BF16),
            pltpu.VMEM((2, reach + 1, rows, d), BF16),
            pltpu.VMEM((reach + 1, rows, d), BF16),
            pltpu.VMEM((reach, rows, d), BF16),
            pltpu.VMEM((reach, rows, d), BF16),
            pltpu.VMEM((cols, d), BF16),
            pltpu.VMEM((cols, d), BF16),
            pltpu.VMEM((rows, d), BF16),
            pltpu.VMEM((plocal, d), BF16),
            dma((2,)), dma((2,)),
            dma, dma((groups,)), dma, dma((groups,)),
            dma, dma((reach,)), dma, dma((reach + 1,)),
            dma, dma((groups,)), dma, dma((reach + 1,)),
            dma, dma, dma, dma((reach,)),
            dma((4,)),
        ],
        compiler_params=pltpu.CompilerParams(
            collective_id=0, has_side_effects=True, vmem_limit_bytes=40 * 1024 * 1024
        ),
    )(queries, response_key_value, prompt_key_value, output_cotangent, lengths)


def solution(mesh):
    spec = P("resp", "head")
    return jax.shard_map(
        shards,
        mesh=mesh,
        in_specs=(spec, spec, spec, spec, P()),
        out_specs=(spec, spec, spec, spec),
        check_vma=False,
    )
```

time: 615 us -> 59.6 us (0.10)
  waiting for transfers between devices: 457 us -> 0 us
  blocking collectives: 67.4 us -> 0 us
  Pallas kernels: 0 us -> 52.3 us
  starting transfers between devices: 47.8 us -> 0 us
  between operations: 14.6 us -> 0.65 us
  matrix products: 12 us -> 0 us
    reduce_scatter x2 -> x0, waiting for transfers between devices: 448 us -> none  [the longest x1 229 us: shards(): lax.psum_scatter(value_full, 'resp', scatter_dimension=0, tiled=True)]
    all_gather x1 -> x0, blocking collectives: 67.4 us -> none  [shards(): gathered = lax.all_gather(prompt_full, 'resp', axis=0, tiled=True)]
    pallas_call x0 -> x1, Pallas kernels: none -> 52.3 us  [shards(): pl.pallas_call(functools.partial(kernel, count), out_shape=(jax.ShapeDtyp...]
    ppermute x14 -> x0, starting transfers between devices: 47.7 us -> none  [the longest x12 31.8 us: from_behind(): return lax.ppermute(x, axis, pairs)]
    dot_general x42 -> x0, matrix products: 12 us -> none  [the longest x8 2.22 us: window_scores(): jnp.einsum('rd,kd->rk', query_head, span_key_rows, preferred_element_type...]
    ppermute x14 -> x0, waiting for transfers between devices: 9.39 us -> none  [the longest x12 8.58 us: from_behind(): return lax.ppermute(x, axis, pairs)]
  transfers between devices with their start and end apart: 16 -> 0, of which waited for: 7 -> 0; matrix products, arithmetic and copies ran while one was open for 1% -> 0% of each run, Pallas kernels for 0% -> 0%
where the time goes in v1:
time: 59.6 us; the launch traced here: 59.3 us
  Pallas kernels  52.3 us (88%)
  local copies, waits for them, and re-layouts  6.35 us (11%)
  between operations  0.65 us (1%)
    pallas_call x1, Pallas kernels, shards(): pl.pallas_call(functools.partial(kernel, count), out_shape=(jax.ShapeDtyp...  52.3 us
    unnamed x14, local copies, waits for them, and re-layouts  6.35 us

profile of v1, /device:TPU:1, one launch (start us, length us, event | category | flops | bytes accessed | tf_op | source)
XLA Modules:
  0.0 59.3 jit_solution(8967089246867528240)
XLA Ops:
  0.6 0.0 copy-start
  0.6 0.9 %copy-done = bf16[96,512]{1,0:T(8,128)(2,1)S(1)} copy-done((bf16[96,512]{1,0:T(8,128)(2,1)S(1)}, bf16[96,512]{1,0:T(8,128)(2,1)}, u32[]{:S(2)}) %copy-start) | copy-done | bytes 98328
  1.5 0.0 copy-start.1
  1.5 0.9 %copy-done.1 = bf16[96,512]{1,0:T(8,128)(2,1)S(1)} copy-done((bf16[96,512]{1,0:T(8,128)(2,1)S(1)}, bf16[96,512]{1,0:T(8,128)(2,1)}, u32[]{:S(2)}) %copy-start.1) | copy-done | bytes 98328
  2.4 0.0 copy-start.2
  2.4 0.7 %copy-done.2 = bf16[96,128]{1,0:T(8,128)(2,1)S(1)} copy-done((bf16[96,128]{1,0:T(8,128)(2,1)S(1)}, bf16[96,128]{1,0:T(8,128)(2,1)}, u32[]{:S(2)}) %copy-start.2) | copy-done | bytes 24600
  3.2 0.0 copy-start.3
  3.2 0.7 %copy-done.3 = bf16[32,128]{1,0:T(8,128)(2,1)S(1)} copy-done((bf16[32,128]{1,0:T(8,128)(2,1)S(1)}, bf16[32,128]{1,0:T(8,128)(2,1)}, u32[]{:S(2)}) %copy-start.3) | copy-done | bytes 8216
  3.9 0.0 copy-start.4
  3.9 0.7 %copy-done.4 = s32[16]{0:T(128)S(1)} copy-done((s32[16]{0:T(128)S(1)}, s32[16]{0:T(128)}, u32[]{:S(2)}) %copy-start.4) | copy-done | bytes 88
  4.5 52.3 %shard_map.84 = (bf16[96,512]{1,0:T(8,128)(2,1)S(1)}, bf16[96,512]{1,0:T(8,128)(2,1)S(1)}, bf16[96,128]{1,0:T(8,128)(2,1)S(1)}, bf16[32,128]{1,0:T(8,128)(2,1)S(1)}) custom-call(bf16[96,512]{1,0:T(8,128)(2,1)S(1)} %copy-done, bf16[96,128]{1,0:T(8,128)(2,1)S(1)} %copy-done.2, bf16[32,128]{1,0:T(8,128)(2,1)S(1)} %copy-done.3, bf16[96,512]{1,0:T(8,128)(2,1)S(1)} %copy-done.1, ...), custom_call_target="tpu_custom_call" | custom-call | tf_op jit(solution)/shard_map/pallas_call | solution.py:303
  56.8 0.6 %copy.13 = bf16[96,512]{1,0:T(8,128)(2,1)} copy(bf16[96,512]{1,0:T(8,128)(2,1)S(1)} %get-tuple-element.8) | data formatting | bytes 196608
  57.4 0.6 %copy.14 = bf16[96,512]{1,0:T(8,128)(2,1)} copy(bf16[96,512]{1,0:T(8,128)(2,1)S(1)} %get-tuple-element.9) | data formatting | bytes 196608
  58.1 0.6 %copy.15 = bf16[96,128]{1,0:T(8,128)(2,1)} copy(bf16[96,128]{1,0:T(8,128)(2,1)S(1)} %get-tuple-element.10) | data formatting | bytes 49152
  58.7 0.6 %copy.16 = bf16[32,128]{1,0:T(8,128)(2,1)} copy(bf16[32,128]{1,0:T(8,128)(2,1)S(1)} %get-tuple-element.11) | data formatting | bytes 16384
Async XLA Ops:
  0.6 0.9 %copy-start = (bf16[96,512]{1,0:T(8,128)(2,1)S(1)}, bf16[96,512]{1,0:T(8,128)(2,1)}, u32[]{:S(2)}) copy-start(bf16[96,512]{1,0:T(8,128)(2,1)} %q_hbm.1) | copy-start | bytes 294916
  1.5 0.9 %copy-start.1 = (bf16[96,512]{1,0:T(8,128)(2,1)S(1)}, bf16[96,512]{1,0:T(8,128)(2,1)}, u32[]{:S(2)}) copy-start(bf16[96,512]{1,0:T(8,128)(2,1)} %do_hbm.1) | copy-start | bytes 294916
  2.4 0.7 %copy-start.2 = (bf16[96,128]{1,0:T(8,128)(2,1)S(1)}, bf16[96,128]{1,0:T(8,128)(2,1)}, u32[]{:S(2)}) copy-start(bf16[96,128]{1,0:T(8,128)(2,1)} %kv_hbm.1) | copy-start | bytes 73732
  3.2 0.7 %copy-start.3 = (bf16[32,128]{1,0:T(8,128)(2,1)S(1)}, bf16[32,128]{1,0:T(8,128)(2,1)}, u32[]{:S(2)}) copy-start(bf16[32,128]{1,0:T(8,128)(2,1)} %pkv_hbm.1) | copy-start | bytes 24580
  3.9 0.7 %copy-start.4 = (s32[16]{0:T(128)S(1)}, s32[16]{0:T(128)}, u32[]{:S(2)}) copy-start(s32[16]{0:T(128)} %len_ref.1) | copy-start | bytes 196

commit v2 on v1

v2 whole, which is shorter than its diff:
```python
import functools
import math

import jax
import jax.numpy as jnp
from jax import lax
from jax.experimental import pallas as pl
from jax.experimental.pallas import tpu as pltpu
from jax.sharding import PartitionSpec as P

MAXLEN = 512
GROUP = 4
AHEAD = 4
BEHIND = 5
MESH = pl.DeviceIdType.MESH
F32 = jnp.float32
BF16 = jnp.bfloat16


def dot(a, b, ca, cb):
    return lax.dot_general(a, b, (((ca,), (cb,)), ((), ())), preferred_element_type=F32)


def wait_bytes(ref, sem):
    pltpu.make_async_copy(ref, ref, sem).wait()


def copy_to(src, dst, send, recv, to):
    pltpu.make_async_remote_copy(
        src_ref=src, dst_ref=dst, send_sem=send, recv_sem=recv, device_id=to, device_id_type=MESH
    ).start()


def at(index, size):
    return pl.ds(pl.multiple_of(index * size, size), size)


def copy_kernel(*refs):
    half = len(refs) // 2
    for i in range(half):
        refs[half + i][...] = refs[i][...]


def window_shape(rows):
    reach = (MAXLEN + rows - 2) // rows
    return reach, -(-(MAXLEN - 1 - (reach - 1) * rows) // 16) * 16


def kernel(
    count,
    q_hbm, kv_hbm, pkv_hbm, do_hbm, len_ref,
    att_hbm, dq_hbm, dkv_hbm, dpkv_hbm,
    qs, dos, kvp, kvw, ebuf, dpbuf, mbuf, wbuf, dsbuf,
    gp, gpin, gpout, rs, gw, gwin, gwout, wr, os, dqs, dkvs, dpkvs,
    load_sem, kv_sem, one_send, a_piece, b_piece, two_send, a_recv, b_recv, pf_send, pf_recv,
    w_send, w_recv, wf_send, wf_recv,
    gx_send, gx_recv, gwx_send, gwx_recv, rs_send, rs_recv, wr_send, wr_recv, out_sem,
):
    rows, width = q_hbm.shape
    d = kv_hbm.shape[1]
    heads = width // d
    cols = heads * rows
    plocal = pkv_hbm.shape[0]
    ny = count // GROUP
    size_a = ny // 2 * plocal
    size_b = GROUP // 2 * plocal
    total_p = count * plocal
    reach, tail = window_shape(rows)
    ahead = tail + (reach - 1) * rows
    scale = 1.0 / math.sqrt(d)
    to_log2 = scale * math.log2(math.e)

    me = lax.axis_index("resp")
    head = lax.axis_index("head")
    kind = lax.rem(head, 2)
    other = 1 - kind
    mate = {"head": head + 1 - 2 * kind}
    y, z = me // GROUP, lax.rem(me, GROUP)

    def device(by, bz):
        return {"resp": lax.rem(y + by, ny) * GROUP + lax.rem(z + bz, GROUP)}

    def peer(by):
        return {"resp": lax.rem(me + by + count, count)}

    odd = lax.rem(y + z, 2)
    own_index = (1 - odd) * (z * (ny // 2) + y // 2) + odd * (
        GROUP * (ny // 2) + y * (GROUP // 2) + z // 2
    )
    own_p = at(own_index, plocal)

    def part_a(pz):
        return at(pz, size_a)

    def part_b(py):
        return pl.ds(pl.multiple_of(GROUP * size_a + py * size_b, size_b), size_b)

    def block(off):
        if off == reach:
            return pl.ds(0, tail)
        return pl.ds(tail + (reach - 1 - off) * rows, rows)

    own_w = block(0)
    z_order = (1, 3, 2)
    y_order = sorted(range(1, ny), key=lambda by: min(by, ny - by))

    kv_copy = pltpu.make_async_copy(kv_hbm, kvw.at[kind, own_w], kv_sem)
    kv_copy.start()

    @pl.when(odd == 0)
    def _():
        pltpu.make_async_copy(pkv_hbm, kvp.at[kind, own_p], a_piece).start()

    @pl.when(odd == 1)
    def _():
        pltpu.make_async_copy(pkv_hbm, kvp.at[kind, own_p], b_piece).start()

    for h in range(heads):
        pltpu.make_async_copy(
            q_hbm.at[:, pl.ds(h * d, d)], qs.at[pl.ds(h * rows, rows)], load_sem.at[0]
        ).start()
        pltpu.make_async_copy(
            do_hbm.at[:, pl.ds(h * d, d)], dos.at[pl.ds(h * rows, rows)], load_sem.at[1]
        ).start()

    barrier = pltpu.get_barrier_semaphore()
    pl.semaphore_signal(barrier, inc=1, device_id=mate, device_id_type=MESH)
    for by in range(1, count):
        pl.semaphore_signal(barrier, inc=1, device_id=peer(by), device_id_type=MESH)
    pl.semaphore_wait(barrier, count)

    @pl.when(odd == 0)
    def _():
        for by in y_order:
            copy_to(pkv_hbm, kvp.at[kind, own_p], one_send.at[0], a_piece, device(by, 0))

    @pl.when(odd == 1)
    def _():
        for bz in z_order:
            copy_to(pkv_hbm, kvp.at[kind, own_p], one_send.at[1], b_piece, device(0, bz))

    kv_copy.wait()
    copy_to(kvw.at[kind, own_w], kvw.at[kind, own_w], wf_send, wf_recv.at[0], mate)
    for off in range(1, reach + 1):
        size = tail if off == reach else rows
        copy_to(
            kvw.at[kind, pl.ds(ahead + rows - size, size)], kvw.at[kind, block(off)],
            w_send, w_recv.at[off - 1], peer(off),
        )

    lane = lax.broadcasted_iota(jnp.int32, (1, cols), 1)
    row_id = lane
    for h in range(1, heads):
        row_id = row_id - jnp.where(lane >= h * rows, rows, 0)
    row_id = row_id + me * rows
    start = jnp.zeros((1, cols), jnp.int32)
    bound = jnp.int32(0)
    for j in range(len_ref.shape[0]):
        length = len_ref[j]
        bound = bound + length
        start = start + jnp.where(bound <= row_id, length, 0)

    wait_bytes(qs, load_sem.at[0])
    wait_bytes(dos, load_sem.at[1])

    stats = [None, None, None]

    def forward(index, keys, values, base, size, off=None):
        s = dot(keys, qs[...], 1, 1) * to_log2
        if off is not None:
            first = me * rows - (ahead if off == reach else off * rows)
            key_id = lax.broadcasted_iota(jnp.int32, (size, cols), 0) + first
            allowed = key_id >= start
            if off == 0:
                allowed = allowed & (key_id <= row_id)
            s = jnp.where(allowed, s, -jnp.inf)
        dp = dot(values, dos[...], 1, 1)
        high = jnp.max(s, axis=0, keepdims=True)
        if stats[0] is not None:
            high = jnp.maximum(high, stats[0])
        e = jnp.exp2(s - high)
        total = jnp.sum(e, axis=0, keepdims=True)
        weighted = jnp.sum(e * dp, axis=0, keepdims=True)
        if stats[0] is not None:
            shrink = jnp.exp2(stats[0] - high)
            total = total + stats[1] * shrink
            weighted = weighted + stats[2] * shrink
        stats[0], stats[1], stats[2] = high, total, weighted
        ebuf[base, :] = e
        dpbuf[base, :] = dp
        mbuf[index] = jnp.broadcast_to(high, (8, cols))

    w_index = GROUP + ny

    def e_block(off):
        rows_at = block(off)
        return pl.ds(total_p + rows_at.start, rows_at.size)

    def forward_window(off):
        wait_bytes(kvw.at[other, block(off)], wf_recv.at[off])
        forward(
            w_index + off, kvw[0, block(off)], kvw[1, block(off)], e_block(off),
            block(off).size, off,
        )

    def index_a(bz):
        return lax.rem(z + bz, GROUP)

    def index_b(by):
        return lax.rem(y + by, ny)

    def forward_a(bz):
        pz = index_a(bz)
        wait_bytes(kvp.at[other, part_a(pz)], pf_recv.at[pz])
        forward(pz, kvp[0, part_a(pz)], kvp[1, part_a(pz)], part_a(pz), size_a)

    def forward_b(by):
        py = index_b(by)
        wait_bytes(kvp.at[other, part_b(py)], pf_recv.at[GROUP + py])
        forward(GROUP + py, kvp[0, part_b(py)], kvp[1, part_b(py)], part_b(py), size_b)

    def pass_a(bz):
        pz = index_a(bz)
        mine = kvp.at[kind, part_a(pz)]
        if bz:
            wait_bytes(mine, a_recv.at[pz])
        copy_to(mine, mine, pf_send, pf_recv.at[pz], mate)

    def pass_b(by):
        py = index_b(by)
        mine = kvp.at[kind, part_b(py)]
        if by:
            wait_bytes(mine, b_recv.at[py])
        copy_to(mine, mine, pf_send, pf_recv.at[GROUP + py], mate)

    def pass_window(off):
        mine = kvw.at[kind, block(off)]
        wait_bytes(mine, w_recv.at[off - 1])
        copy_to(mine, mine, wf_send, wf_recv.at[off], mate)

    forward_window(0)
    mine_b = kvp.at[kind, part_b(y)]
    wait_bytes(mine_b, b_piece)
    for by in y_order:
        copy_to(mine_b, mine_b, two_send, b_recv.at[y], device(by, 0))
    mine_a = kvp.at[kind, part_a(z)]
    wait_bytes(mine_a, a_piece)
    for bz in z_order:
        copy_to(mine_a, mine_a, two_send, a_recv.at[z], device(0, bz))

    steps = [(pass_b, forward_b, 0), (pass_a, forward_a, 0)]
    steps += [(pass_window, forward_window, off) for off in (1, 4, 3, 2, 5, 6)[-reach:]]
    steps += [(pass_b, forward_b, by) for by in y_order[:2]]
    steps += [(pass_a, forward_a, bz) for bz in z_order[:2]]
    steps += [(pass_b, forward_b, by) for by in y_order[2:4]]
    steps += [(pass_a, forward_a, bz) for bz in z_order[2:]]
    steps += [(pass_b, forward_b, by) for by in y_order[4:]]
    for i in range(len(steps) + AHEAD):
        if i < len(steps):
            steps[i][0](steps[i][2])
        if i >= AHEAD:
            steps[i - AHEAD][1](steps[i - AHEAD][2])

    high, total, weighted = stats
    inverse = 1.0 / total
    delta = weighted * inverse

    def backward(index, base):
        factor = jnp.exp2(mbuf[index][:1] - high) * inverse
        w = ebuf[base, :] * factor
        wb = w.astype(BF16)
        ds = (w * (dpbuf[base, :] - delta)).astype(BF16)
        wbuf[base, :] = wb
        dsbuf[base, :] = ds
        return dot(ds, qs[...], 1, 0) * scale, dot(wb, dos[...], 1, 0)

    def backward_prompt(index, rows_at):
        dk, dv = backward(index, rows_at)
        gp[0, rows_at] = dk.astype(BF16)
        gp[1, rows_at] = dv.astype(BF16)
        copy_to(gp.at[other, rows_at], gpin.at[rows_at], gx_send, gx_recv.at[index], mate)

    def finish_prompt(index, rows_at, pieces, holds_own):
        wait_bytes(gpin.at[rows_at], gx_recv.at[index])
        gpout[rows_at, :] = (gp[kind, rows_at].astype(F32) + gpin[rows_at, :].astype(F32)).astype(BF16)
        for j, to in pieces:
            src = gpout.at[pl.ds(pl.multiple_of(rows_at.start + j * plocal, plocal), plocal)]
            if not holds_own:
                copy_to(src, rs.at[me], rs_send, rs_recv, {"resp": to})
                continue

            @pl.when(to != me)
            def _():
                copy_to(src, rs.at[me], rs_send, rs_recv, {"resp": to})

    def backward_a(bz):
        pz = index_a(bz)
        backward_prompt(pz, part_a(pz))

    def backward_b(by):
        py = index_b(by)
        backward_prompt(GROUP + py, part_b(py))

    def finish_a(bz):
        pz = index_a(bz)
        turn = [lax.rem(y // 2 + j, ny // 2) for j in range(ny // 2)]
        pieces = [(j, (2 * j + lax.rem(pz, 2)) * GROUP + pz) for j in turn]
        finish_prompt(pz, part_a(pz), pieces, bz == 0)

    def finish_b(by):
        py = index_b(by)
        pieces = [(j, py * GROUP + 2 * j + 1 - lax.rem(py, 2)) for j in range(GROUP // 2)]
        finish_prompt(GROUP + py, part_b(py), pieces, by == 0)

    def backward_window(off):
        dk, dv = backward(w_index + off, e_block(off))
        gw[0, block(off)] = dk.astype(BF16)
        gw[1, block(off)] = dv.astype(BF16)
        copy_to(gw.at[other, block(off)], gwin.at[block(off)], gwx_send, gwx_recv.at[off], mate)

    def finish_window(off):
        wait_bytes(gwin.at[block(off)], gwx_recv.at[off])
        both = gw[kind, block(off)].astype(F32) + gwin[block(off), :].astype(F32)
        if off == 0:
            return both
        gwout[block(off), :] = both.astype(BF16)
        size = block(off).size
        copy_to(
            gwout.at[block(off)], wr.at[off - 1, pl.ds(0, size)], wr_send, wr_recv.at[off - 1],
            peer(-off),
        )
        return None

    far_y = y_order[::-1]
    back = [(backward_a, finish_a, bz) for bz in (2, 1, 3)]
    back += [(backward_window, finish_window, off) for off in range(reach, reach - 3, -1)]
    back += [(backward_b, finish_b, by) for by in far_y[:4]]
    back += [(backward_window, finish_window, off) for off in range(reach - 3, 0, -1)]
    back += [(backward_b, finish_b, by) for by in far_y[4:]]
    back += [(backward_a, finish_a, 0), (backward_b, finish_b, 0)]
    back.append((backward_window, finish_window, 0))
    for i in range(len(back) + BEHIND):
        if i < len(back):
            back[i][0](back[i][2])
        if i >= BEHIND:
            own_grad = back[i - BEHIND][1](back[i - BEHIND][2])
    rs[me] = gpout[own_p, :]

    p_part = pl.ds(0, total_p)
    w_part = pl.ds(total_p, ahead + rows)
    out_t = dot(kvp[1], wbuf[p_part, :], 0, 0) + dot(kvw[1], wbuf[w_part, :], 0, 0)
    os[...] = out_t.T.astype(BF16)
    for h in range(heads):
        pltpu.make_async_copy(
            os.at[pl.ds(h * rows, rows)], att_hbm.at[:, pl.ds(h * d, d)], out_sem.at[0]
        ).start()
    dq_t = dot(kvp[0], dsbuf[p_part, :], 0, 0) + dot(kvw[0], dsbuf[w_part, :], 0, 0)
    dqs[...] = (dq_t.T * scale).astype(BF16)
    for h in range(heads):
        pltpu.make_async_copy(
            dqs.at[pl.ds(h * rows, rows)], dq_hbm.at[:, pl.ds(h * d, d)], out_sem.at[1]
        ).start()

    for off in range(1, reach):
        wait_bytes(wr.at[off - 1], wr_recv.at[off - 1])
        own_grad = own_grad + wr[off - 1].astype(F32)
    far = wr.at[reach - 1, pl.ds(0, tail)]
    wait_bytes(far, wr_recv.at[reach - 1])
    own_grad = jnp.concatenate(
        [own_grad[: rows - tail], own_grad[rows - tail :] + far[...].astype(F32)], axis=0
    )
    dkvs[...] = own_grad.astype(BF16)
    dkv_copy = pltpu.make_async_copy(dkvs, dkv_hbm, out_sem.at[2])
    dkv_copy.start()
    wait_bytes(rs.at[pl.ds(0, count - 1)], rs_recv)
    dpkvs[...] = jnp.sum(rs[...].astype(F32), axis=0).astype(BF16)
    dpkv_copy = pltpu.make_async_copy(dpkvs, dpkv_hbm, out_sem.at[3])
    dpkv_copy.start()

    @pl.when(odd == 0)
    def _():
        wait_bytes(kvp.at[0, pl.ds(0, (ny - 1) * plocal)], one_send.at[0])

    @pl.when(odd == 1)
    def _():
        wait_bytes(kvp.at[0, pl.ds(0, (GROUP - 1) * plocal)], one_send.at[1])

    wait_bytes(kvp.at[0, pl.ds(0, (GROUP - 1) * size_a + (ny - 1) * size_b)], two_send)
    wait_bytes(kvp.at[0], pf_send)
    wait_bytes(kvw.at[0, pl.ds(0, ahead)], w_send)
    wait_bytes(kvw.at[0], wf_send)
    wait_bytes(gpin, gx_send)
    wait_bytes(gwin, gwx_send)
    wait_bytes(rs.at[pl.ds(0, count - 1)], rs_send)
    wait_bytes(gwout.at[pl.ds(0, ahead)], wr_send)
    wait_bytes(os, out_sem.at[0])
    wait_bytes(dqs, out_sem.at[1])
    dkv_copy.wait()
    dpkv_copy.wait()


def shards(queries, response_key_value, prompt_key_value, output_cotangent, lengths):
    rows, width = queries.shape
    d = response_key_value.shape[1]
    cols = width // d * rows
    plocal = prompt_key_value.shape[0]
    count = lax.axis_size("resp")
    total_p = plocal * count
    ny = count // GROUP
    reach, tail = window_shape(rows)
    window = tail + reach * rows
    keys = total_p + window
    dma, anywhere = pltpu.SemaphoreType.DMA, pl.BlockSpec(memory_space=pl.ANY)
    whole = pl.BlockSpec(memory_space=pltpu.VMEM)
    limit = 60 * 1024 * 1024
    out_shape = (
        jax.ShapeDtypeStruct(queries.shape, BF16),
        jax.ShapeDtypeStruct(queries.shape, BF16),
        jax.ShapeDtypeStruct(response_key_value.shape, BF16),
        jax.ShapeDtypeStruct(prompt_key_value.shape, BF16),
    )
    results = pl.pallas_call(
        functools.partial(kernel, count),
        out_shape=out_shape,
        in_specs=[anywhere] * 4 + [pl.BlockSpec(memory_space=pltpu.SMEM)],
        out_specs=(anywhere,) * 4,
        scratch_shapes=[
            pltpu.VMEM((cols, d), BF16),
            pltpu.VMEM((cols, d), BF16),
            pltpu.VMEM((2, total_p, d), BF16),
            pltpu.VMEM((2, window, d), BF16),
            pltpu.VMEM((keys, cols), F32),
            pltpu.VMEM((keys, cols), F32),
            pltpu.VMEM((GROUP + ny + reach + 1, 8, cols), F32),
            pltpu.VMEM((keys, cols), BF16),
            pltpu.VMEM((keys, cols), BF16),
            pltpu.VMEM((2, total_p, d), BF16),
            pltpu.VMEM((total_p, d), BF16),
            pltpu.VMEM((total_p, d), BF16),
            pltpu.VMEM((count, plocal, d), BF16),
            pltpu.VMEM((2, window, d), BF16),
            pltpu.VMEM((window, d), BF16),
            pltpu.VMEM((window, d), BF16),
            pltpu.VMEM((reach, rows, d), BF16),
            pltpu.VMEM((cols, d), BF16),
            pltpu.VMEM((cols, d), BF16),
            pltpu.VMEM((rows, d), BF16),
            pltpu.VMEM((plocal, d), BF16),
            dma((2,)), dma, dma((2,)), dma, dma, dma, dma((GROUP,)), dma((ny,)),
            dma, dma((GROUP + ny,)),
            dma, dma((reach,)), dma, dma((reach + 1,)),
            dma, dma((GROUP + ny,)), dma, dma((reach + 1,)),
            dma, dma, dma, dma((reach,)),
            dma((4,)),
        ],
        compiler_params=pltpu.CompilerParams(
            collective_id=0, has_side_effects=True, vmem_limit_bytes=limit
        ),
    )(queries, response_key_value, prompt_key_value, output_cotangent, lengths)
    return pl.pallas_call(
        copy_kernel,
        out_shape=out_shape,
        in_specs=[whole] * 4,
        out_specs=(whole,) * 4,
        compiler_params=pltpu.CompilerParams(vmem_limit_bytes=limit),
    )(*results)


def solution(mesh):
    spec = P("resp", "head")
    return jax.shard_map(
        shards,
        mesh=mesh,
        in_specs=(spec, spec, spec, spec, P()),
        out_specs=(spec, spec, spec, spec),
        check_vma=False,
    )
```

time: 59.6 us -> 46.8 us (0.79)
  Pallas kernels: 52.3 us -> 45.9 us
  local copies, waits for them, and re-layouts: 6.35 us -> 0 us
    unnamed x14 -> x0, local copies, waits for them, and re-layouts: 6.35 us -> none
    pallas_call x1 -> x2, Pallas kernels: 52.3 us -> 45.9 us  [the longest x1 44.3 us: shards(): pl.pallas_call(functools.partial(kernel, count), out_shape=out_shape, in_...]
where the time goes in v2:
time: 46.8 us; the launch traced here: 46.6 us
  Pallas kernels  45.9 us (98%)
  between operations  0.64 us (1%)
    pallas_call x1, Pallas kernels, shards(): pl.pallas_call(functools.partial(kernel, count), out_shape=out_shape, in_...  44.3 us
    pallas_call x1, Pallas kernels, shards(): pl.pallas_call(copy_kernel, out_shape=out_shape, in_specs=[whole] * 4, ou...  1.63 us

profile of v2, /device:TPU:1, one launch (start us, length us, event | category | flops | bytes accessed | tf_op | source)
XLA Modules:
  0.0 46.6 jit_solution(15282245778925473579)
XLA Ops:
  0.6 44.3 %shard_map.84 = (bf16[96,512]{1,0:T(8,128)(2,1)}, bf16[96,512]{1,0:T(8,128)(2,1)}, bf16[96,128]{1,0:T(8,128)(2,1)}, bf16[32,128]{1,0:T(8,128)(2,1)}) custom-call(bf16[96,512]{1,0:T(8,128)(2,1)} %q_hbm.1, bf16[96,128]{1,0:T(8,128)(2,1)} %kv_hbm.1, bf16[32,128]{1,0:T(8,128)(2,1)} %pkv_hbm.1, bf16[96,512]{1,0:T(8,128)(2,1)} %do_hbm.1, s32[16]{0:T(128)} %len_ref.1), custom_call_target="tpu_custom_call" | custom-call | tf_op jit(solution)/shard_map/pallas_call | solution.py:422
  44.9 1.6 %shard_map.85 = (bf16[96,512]{1,0:T(8,128)(2,1)}, bf16[96,512]{1,0:T(8,128)(2,1)}, bf16[96,128]{1,0:T(8,128)(2,1)}, bf16[32,128]{1,0:T(8,128)(2,1)}) custom-call(bf16[96,512]{1,0:T(8,128)(2,1)} %get-tuple-element.8.refs_0_, bf16[96,512]{1,0:T(8,128)(2,1)} %get-tuple-element.9.refs_1_, bf16[96,128]{1,0:T(8,128)(2,1)} %get-tuple-element.10.refs_2_, ...), custom_call_target="tpu_custom_call" | custom-call | tf_op jit(solution)/shard_map/pallas_call | solution.py:460

commit v3 on v2

--- a/solution.py
+++ b/solution.py
@@ -10,8 +10,8 @@
 
 MAXLEN = 512
 GROUP = 4
-AHEAD = 4
-BEHIND = 5
+AHEAD = 2
+BEHIND = 3
 MESH = pl.DeviceIdType.MESH
 F32 = jnp.float32
 BF16 = jnp.bfloat16
@@ -49,12 +49,12 @@
 def kernel(
     count,
     q_hbm, kv_hbm, pkv_hbm, do_hbm, len_ref,
-    att_hbm, dq_hbm, dkv_hbm, dpkv_hbm,
+    att_ref, dq_ref, dkv_ref, dpkv_ref,
     qs, dos, kvp, kvw, ebuf, dpbuf, mbuf, wbuf, dsbuf,
-    gp, gpin, gpout, rs, gw, gwin, gwout, wr, os, dqs, dkvs, dpkvs,
+    gp, gpin, gpout, rs, gw, gwin, gwout, wr,
     load_sem, kv_sem, one_send, a_piece, b_piece, two_send, a_recv, b_recv, pf_send, pf_recv,
     w_send, w_recv, wf_send, wf_recv,
-    gx_send, gx_recv, gwx_send, gwx_recv, rs_send, rs_recv, wr_send, wr_recv, out_sem,
+    gx_send, gx_recv, gwx_send, gwx_recv, rs_send, rs_recv, wr_send, wr_recv,
 ):
     rows, width = q_hbm.shape
     d = kv_hbm.shape[1]
@@ -64,7 +64,6 @@
     ny = count // GROUP
     size_a = ny // 2 * plocal
     size_b = GROUP // 2 * plocal
-    total_p = count * plocal
     reach, tail = window_shape(rows)
     ahead = tail + (reach - 1) * rows
     scale = 1.0 / math.sqrt(d)
@@ -107,14 +106,8 @@
     kv_copy = pltpu.make_async_copy(kv_hbm, kvw.at[kind, own_w], kv_sem)
     kv_copy.start()
 
-    @pl.when(odd == 0)
-    def _():
-        pltpu.make_async_copy(pkv_hbm, kvp.at[kind, own_p], a_piece).start()
-
-    @pl.when(odd == 1)
-    def _():
-        pltpu.make_async_copy(pkv_hbm, kvp.at[kind, own_p], b_piece).start()
-
+    own_copy = pltpu.make_async_copy(pkv_hbm, kvp.at[kind, own_p], load_sem.at[2])
+    own_copy.start()
     for h in range(heads):
         pltpu.make_async_copy(
             q_hbm.at[:, pl.ds(h * d, d)], qs.at[pl.ds(h * rows, rows)], load_sem.at[0]
@@ -124,20 +117,32 @@
         ).start()
 
     barrier = pltpu.get_barrier_semaphore()
+    greeted = [device(by, 0) for by in y_order] + [device(0, bz) for bz in z_order]
+    greeted += [peer(by) for off in range(1, reach + 1) if off % GROUP for by in (off, -off)]
     pl.semaphore_signal(barrier, inc=1, device_id=mate, device_id_type=MESH)
-    for by in range(1, count):
-        pl.semaphore_signal(barrier, inc=1, device_id=peer(by), device_id_type=MESH)
-    pl.semaphore_wait(barrier, count)
+    for to in greeted:
+        pl.semaphore_signal(barrier, inc=1, device_id=to, device_id_type=MESH)
+    pl.semaphore_wait(barrier, len(greeted) + 1)
+
+    def send_along_y(rows_at, send, arrived):
+        for by in y_order:
+            copy_to(kvp.at[kind, rows_at], kvp.at[kind, rows_at], send, arrived, device(by, 0))
+
+    def send_along_z(rows_at, send, arrived):
+        for bz in z_order:
+            copy_to(kvp.at[kind, rows_at], kvp.at[kind, rows_at], send, arrived, device(0, bz))
+
+    own_copy.wait()
 
     @pl.when(odd == 0)
     def _():
-        for by in y_order:
-            copy_to(pkv_hbm, kvp.at[kind, own_p], one_send.at[0], a_piece, device(by, 0))
+        send_along_y(own_p, one_send.at[0], a_piece.at[y // 2])
+        send_along_z(own_p, two_send, a_recv.at[z])
 
     @pl.when(odd == 1)
     def _():
-        for bz in z_order:
-            copy_to(pkv_hbm, kvp.at[kind, own_p], one_send.at[1], b_piece, device(0, bz))
+        send_along_z(own_p, one_send.at[1], b_piece.at[z // 2])
+        send_along_y(own_p, two_send, b_recv.at[y])
 
     kv_copy.wait()
     copy_to(kvw.at[kind, own_w], kvw.at[kind, own_w], wf_send, wf_recv.at[0], mate)
@@ -165,16 +170,18 @@
 
     stats = [None, None, None]
 
-    def forward(index, keys, values, base, size, off=None):
+    def forward(index, sources, off=None):
+        keys = jnp.concatenate([buffer[0, at_rows] for buffer, at_rows, _, _ in sources], axis=0)
+        values = jnp.concatenate([buffer[1, at_rows] for buffer, at_rows, _, _ in sources], axis=0)
         s = dot(keys, qs[...], 1, 1) * to_log2
-        if off is not None:
-            first = me * rows - (ahead if off == reach else off * rows)
-            key_id = lax.broadcasted_iota(jnp.int32, (size, cols), 0) + first
-            allowed = key_id >= start
-            if off == 0:
-                allowed = allowed & (key_id <= row_id)
-            s = jnp.where(allowed, s, -jnp.inf)
         dp = dot(values, dos[...], 1, 1)
+        if sources[0][3] is not None:
+            masks = []
+            for _, at_rows, _, off in sources:
+                first = me * rows - (ahead if off == reach else off * rows)
+                key_id = lax.broadcasted_iota(jnp.int32, (at_rows.size, cols), 0) + first
+                masks.append((key_id >= start) & (key_id <= row_id))
+            s = jnp.where(jnp.concatenate(masks, axis=0), s, -jnp.inf)
         high = jnp.max(s, axis=0, keepdims=True)
         if stats[0] is not None:
             high = jnp.maximum(high, stats[0])
@@ -186,38 +193,46 @@
             total = total + stats[1] * shrink
             weighted = weighted + stats[2] * shrink
         stats[0], stats[1], stats[2] = high, total, weighted
-        ebuf[base, :] = e
-        dpbuf[base, :] = dp
+        done = 0
+        for _, _, base, _ in sources:
+            ebuf[base, :] = e[done : done + base.size]
+            dpbuf[base, :] = dp[done : done + base.size]
+            done += base.size
         mbuf[index] = jnp.broadcast_to(high, (8, cols))
 
-    w_index = GROUP + ny
+    total_p = count * plocal
 
     def e_block(off):
         rows_at = block(off)
         return pl.ds(total_p + rows_at.start, rows_at.size)
 
-    def forward_window(off):
-        wait_bytes(kvw.at[other, block(off)], wf_recv.at[off])
-        forward(
-            w_index + off, kvw[0, block(off)], kvw[1, block(off)], e_block(off),
-            block(off).size, off,
-        )
-
     def index_a(bz):
         return lax.rem(z + bz, GROUP)
 
     def index_b(by):
         return lax.rem(y + by, ny)
 
-    def forward_a(bz):
-        pz = index_a(bz)
-        wait_bytes(kvp.at[other, part_a(pz)], pf_recv.at[pz])
-        forward(pz, kvp[0, part_a(pz)], kvp[1, part_a(pz)], part_a(pz), size_a)
-
-    def forward_b(by):
-        py = index_b(by)
-        wait_bytes(kvp.at[other, part_b(py)], pf_recv.at[GROUP + py])
-        forward(GROUP + py, kvp[0, part_b(py)], kvp[1, part_b(py)], part_b(py), size_b)
+    def source(item):
+        what, n = item
+        if what == "a":
+            return kvp, part_a(index_a(n)), part_a(index_a(n)), None
+        if what == "b":
+            return kvp, part_b(index_b(n)), part_b(index_b(n)), None
+        return kvw, block(n), e_block(n), n
+
+    def passed(item):
+        what, n = item
+        if what == "a":
+            return pf_recv.at[index_a(n)]
+        if what == "b":
+            return pf_recv.at[GROUP + index_b(n)]
+        return wf_recv.at[n]
+
+    def forward_group(index):
+        for item in groups[index]:
+            buffer, at_rows, _, _ = source(item)
+            wait_bytes(buffer.at[other, at_rows], passed(item))
+        forward(index, [source(item) for item in groups[index]])
 
     def pass_a(bz):
         pz = index_a(bz)
@@ -238,47 +253,79 @@
         wait_bytes(mine, w_recv.at[off - 1])
         copy_to(mine, mine, wf_send, wf_recv.at[off], mate)
 
-    forward_window(0)
-    mine_b = kvp.at[kind, part_b(y)]
-    wait_bytes(mine_b, b_piece)
-    for by in y_order:
-        copy_to(mine_b, mine_b, two_send, b_recv.at[y], device(by, 0))
-    mine_a = kvp.at[kind, part_a(z)]
-    wait_bytes(mine_a, a_piece)
-    for bz in z_order:
-        copy_to(mine_a, mine_a, two_send, a_recv.at[z], device(0, bz))
-
-    steps = [(pass_b, forward_b, 0), (pass_a, forward_a, 0)]
-    steps += [(pass_window, forward_window, off) for off in (1, 4, 3, 2, 5, 6)[-reach:]]
-    steps += [(pass_b, forward_b, by) for by in y_order[:2]]
-    steps += [(pass_a, forward_a, bz) for bz in z_order[:2]]
-    steps += [(pass_b, forward_b, by) for by in y_order[2:4]]
-    steps += [(pass_a, forward_a, bz) for bz in z_order[2:]]
-    steps += [(pass_b, forward_b, by) for by in y_order[4:]]
-    for i in range(len(steps) + AHEAD):
-        if i < len(steps):
-            steps[i][0](steps[i][2])
-        if i >= AHEAD:
-            steps[i - AHEAD][1](steps[i - AHEAD][2])
+    passes = {"a": pass_a, "b": pass_b, "w": pass_window}
+    groups = [[("w", 0)], [("b", 0), ("a", 0)]]
+    groups += [[("w", off) for off in offs] for offs in ((1, 4), (3, 2), (5, 6))]
+    pairs = [[("b", by) for by in y_order[i : i + 2]] for i in range(0, max(len(y_order) - 1, 1), 2)]
+    if len(y_order) > 1:
+        pairs[-1].append(("b", y_order[-1]))
+    groups += pairs[:1] + [[("a", bz)] for bz in z_order[:2]] + pairs[1:2]
+    groups += [[("a", bz)] for bz in z_order[2:]] + pairs[2:]
+
+    forward_group(0)
+    def pass_on_a(by):
+        place = lax.rem(y + by, ny) // 2
+        rows_at = at(z * (ny // 2) + place, plocal)
+        wait_bytes(kvp.at[kind, rows_at], a_piece.at[place])
+        send_along_z(rows_at, two_send, a_recv.at[z])
+
+    def pass_on_b(bz):
+        place = lax.rem(z + bz, GROUP) // 2
+        rows_at = at(GROUP * (ny // 2) + y * (GROUP // 2) + place, plocal)
+        wait_bytes(kvp.at[kind, rows_at], b_piece.at[place])
+        send_along_y(rows_at, two_send, b_recv.at[y])
+
+    @pl.when(odd == 0)
+    def _():
+        for bz in (1, 3):
+            pass_on_b(bz)
+        for by in y_order:
+            if by % 2 == 0:
+                pass_on_a(by)
+
+    @pl.when(odd == 1)
+    def _():
+        for by in y_order:
+            if by % 2 == 1:
+                pass_on_a(by)
+        pass_on_b(2)
+
+    for i in range(1, len(groups) + AHEAD):
+        if i < len(groups):
+            for what, n in groups[i]:
+                passes[what](n)
+        if i > AHEAD:
+            forward_group(i - AHEAD)
 
     high, total, weighted = stats
     inverse = 1.0 / total
     delta = weighted * inverse
 
-    def backward(index, base):
+    def backward(index):
+        sources = [source(item) for item in groups[index]]
         factor = jnp.exp2(mbuf[index][:1] - high) * inverse
-        w = ebuf[base, :] * factor
+        w = jnp.concatenate([ebuf[base, :] for _, _, base, _ in sources], axis=0) * factor
+        dp = jnp.concatenate([dpbuf[base, :] for _, _, base, _ in sources], axis=0)
         wb = w.astype(BF16)
-        ds = (w * (dpbuf[base, :] - delta)).astype(BF16)
-        wbuf[base, :] = wb
-        dsbuf[base, :] = ds
-        return dot(ds, qs[...], 1, 0) * scale, dot(wb, dos[...], 1, 0)
-
-    def backward_prompt(index, rows_at):
-        dk, dv = backward(index, rows_at)
-        gp[0, rows_at] = dk.astype(BF16)
-        gp[1, rows_at] = dv.astype(BF16)
-        copy_to(gp.at[other, rows_at], gpin.at[rows_at], gx_send, gx_recv.at[index], mate)
+        ds = (w * (dp - delta)).astype(BF16)
+        dk = (dot(ds, qs[...], 1, 0) * scale).astype(BF16)
+        dv = dot(wb, dos[...], 1, 0).astype(BF16)
+        done = 0
+        for item, (buffer, at_rows, base, _) in zip(groups[index], sources):
+            now = slice(done, done + base.size)
+            done += base.size
+            wbuf[base, :] = wb[now]
+            dsbuf[base, :] = ds[now]
+            own, received, send, arrived = grads(item)
+            own[0, at_rows] = dk[now]
+            own[1, at_rows] = dv[now]
+            copy_to(own.at[other, at_rows], received.at[at_rows], send, arrived, mate)
+
+    def grads(item):
+        what, n = item
+        if what == "w":
+            return gw, gwin, gwx_send, gwx_recv.at[n]
+        return gp, gpin, gx_send, gx_recv.at[index_a(n) if what == "a" else GROUP + index_b(n)]
 
     def finish_prompt(index, rows_at, pieces, holds_own):
         wait_bytes(gpin.at[rows_at], gx_recv.at[index])
@@ -293,14 +340,6 @@
             def _():
                 copy_to(src, rs.at[me], rs_send, rs_recv, {"resp": to})
 
-    def backward_a(bz):
-        pz = index_a(bz)
-        backward_prompt(pz, part_a(pz))
-
-    def backward_b(by):
-        py = index_b(by)
-        backward_prompt(GROUP + py, part_b(py))
-
     def finish_a(bz):
         pz = index_a(bz)
         turn = [lax.rem(y // 2 + j, ny // 2) for j in range(ny // 2)]
@@ -311,12 +350,6 @@
         py = index_b(by)
         pieces = [(j, py * GROUP + 2 * j + 1 - lax.rem(py, 2)) for j in range(GROUP // 2)]
         finish_prompt(GROUP + py, part_b(py), pieces, by == 0)
-
-    def backward_window(off):
-        dk, dv = backward(w_index + off, e_block(off))
-        gw[0, block(off)] = dk.astype(BF16)
-        gw[1, block(off)] = dv.astype(BF16)
-        copy_to(gw.at[other, block(off)], gwin.at[block(off)], gwx_send, gwx_recv.at[off], mate)
 
     def finish_window(off):
         wait_bytes(gwin.at[block(off)], gwx_recv.at[off])
@@ -331,35 +364,26 @@
         )
         return None
 
-    far_y = y_order[::-1]
-    back = [(backward_a, finish_a, bz) for bz in (2, 1, 3)]
-    back += [(backward_window, finish_window, off) for off in range(reach, reach - 3, -1)]
-    back += [(backward_b, finish_b, by) for by in far_y[:4]]
-    back += [(backward_window, finish_window, off) for off in range(reach - 3, 0, -1)]
-    back += [(backward_b, finish_b, by) for by in far_y[4:]]
-    back += [(backward_a, finish_a, 0), (backward_b, finish_b, 0)]
-    back.append((backward_window, finish_window, 0))
+    finishes = {"a": finish_a, "b": finish_b, "w": finish_window}
+    back = list(range(len(groups) - 1, -1, -1))
     for i in range(len(back) + BEHIND):
         if i < len(back):
-            back[i][0](back[i][2])
+            backward(back[i])
         if i >= BEHIND:
-            own_grad = back[i - BEHIND][1](back[i - BEHIND][2])
+            for what, n in groups[back[i - BEHIND]]:
+                own_grad = finishes[what](n)
     rs[me] = gpout[own_p, :]
 
     p_part = pl.ds(0, total_p)
     w_part = pl.ds(total_p, ahead + rows)
     out_t = dot(kvp[1], wbuf[p_part, :], 0, 0) + dot(kvw[1], wbuf[w_part, :], 0, 0)
-    os[...] = out_t.T.astype(BF16)
+    out = out_t.T.astype(BF16)
     for h in range(heads):
-        pltpu.make_async_copy(
-            os.at[pl.ds(h * rows, rows)], att_hbm.at[:, pl.ds(h * d, d)], out_sem.at[0]
-        ).start()
+        att_ref[:, h * d : (h + 1) * d] = out[h * rows : (h + 1) * rows]
     dq_t = dot(kvp[0], dsbuf[p_part, :], 0, 0) + dot(kvw[0], dsbuf[w_part, :], 0, 0)
-    dqs[...] = (dq_t.T * scale).astype(BF16)
+    dq = (dq_t.T * scale).astype(BF16)
     for h in range(heads):
-        pltpu.make_async_copy(
-            dqs.at[pl.ds(h * rows, rows)], dq_hbm.at[:, pl.ds(h * d, d)], out_sem.at[1]
-        ).start()
+        dq_ref[:, h * d : (h + 1) * d] = dq[h * rows : (h + 1) * rows]
 
     for off in range(1, reach):
         wait_bytes(wr.at[off - 1], wr_recv.at[off - 1])
@@ -369,13 +393,9 @@
     own_grad = jnp.concatenate(
         [own_grad[: rows - tail], own_grad[rows - tail :] + far[...].astype(F32)], axis=0
     )
-    dkvs[...] = own_grad.astype(BF16)
-    dkv_copy = pltpu.make_async_copy(dkvs, dkv_hbm, out_sem.at[2])
-    dkv_copy.start()
+    dkv_ref[...] = own_grad.astype(BF16)
     wait_bytes(rs.at[pl.ds(0, count - 1)], rs_recv)
-    dpkvs[...] = jnp.sum(rs[...].astype(F32), axis=0).astype(BF16)
-    dpkv_copy = pltpu.make_async_copy(dpkvs, dpkv_hbm, out_sem.at[3])
-    dpkv_copy.start()
+    dpkv_ref[...] = jnp.sum(rs[...].astype(F32), axis=0).astype(BF16)
 
     @pl.when(odd == 0)
     def _():
@@ -393,10 +413,6 @@
     wait_bytes(gwin, gwx_send)
     wait_bytes(rs.at[pl.ds(0, count - 1)], rs_send)
     wait_bytes(gwout.at[pl.ds(0, ahead)], wr_send)
-    wait_bytes(os, out_sem.at[0])
-    wait_bytes(dqs, out_sem.at[1])
-    dkv_copy.wait()
-    dpkv_copy.wait()
 
 
 def shards(queries, response_key_value, prompt_key_value, output_cotangent, lengths):
@@ -421,9 +437,9 @@
     )
     results = pl.pallas_call(
         functools.partial(kernel, count),
-        out_shape=out_shape,
+        out_shape=tuple(pltpu.VMEM(s.shape, s.dtype) for s in out_shape),
         in_specs=[anywhere] * 4 + [pl.BlockSpec(memory_space=pltpu.SMEM)],
-        out_specs=(anywhere,) * 4,
+        out_specs=(whole,) * 4,
         scratch_shapes=[
             pltpu.VMEM((cols, d), BF16),
             pltpu.VMEM((cols, d), BF16),
@@ -442,16 +458,12 @@
             pltpu.VMEM((window, d), BF16),
             pltpu.VMEM((window, d), BF16),
             pltpu.VMEM((reach, rows, d), BF16),
-            pltpu.VMEM((cols, d), BF16),
-            pltpu.VMEM((cols, d), BF16),
-            pltpu.VMEM((rows, d), BF16),
-            pltpu.VMEM((plocal, d), BF16),
-            dma((2,)), dma, dma((2,)), dma, dma, dma, dma((GROUP,)), dma((ny,)),
+            dma((3,)), dma, dma((2,)), dma((ny // 2,)), dma((GROUP // 2,)), dma, dma((GROUP,)),
+            dma((ny,)),
             dma, dma((GROUP + ny,)),
             dma, dma((reach,)), dma, dma((reach + 1,)),
             dma, dma((GROUP + ny,)), dma, dma((reach + 1,)),
             dma, dma, dma, dma((reach,)),
-            dma((4,)),
         ],
         compiler_params=pltpu.CompilerParams(
             collective_id=0, has_side_effects=True, vmem_limit_bytes=limit
@@ -463,7 +475,7 @@
         in_specs=[whole] * 4,
         out_specs=(whole,) * 4,
         compiler_params=pltpu.CompilerParams(vmem_limit_bytes=limit),
-    )(*results)
+    )(*[pltpu.with_memory_space_constraint(r, pltpu.VMEM) for r in results])
 
 
 def solution(mesh):

time: 46.8 us -> 43.9 us (0.938)
  Pallas kernels: 45.9 us -> 43.1 us
    pallas_call x1, Pallas kernels: 44.3 us -> 42.4 us  [shards(): pl.pallas_call(functools.partial(kernel, count), out_shape=tuple((pltpu.V...]
    pallas_call x1, Pallas kernels: 1.63 us -> 0.69 us  [shards(): pl.pallas_call(copy_kernel, out_shape=out_shape, in_specs=[whole] * 4, ou...]
where the time goes in v3:
time: 43.9 us; the launch traced here: 43.8 us
  Pallas kernels  43.1 us (98%)
  between operations  0.64 us (1%)
    pallas_call x1, Pallas kernels, shards(): pl.pallas_call(functools.partial(kernel, count), out_shape=tuple((pltpu.V...  42.4 us

profile of v3, /device:TPU:1, one launch (start us, length us, event | category | flops | bytes accessed | tf_op | source)
XLA Modules:
  0.0 43.8 jit_solution(16970072807429852449)
XLA Ops:
  0.6 42.4 %shard_map.84 = (bf16[96,512]{1,0:T(8,128)(2,1)S(1)}, bf16[96,512]{1,0:T(8,128)(2,1)S(1)}, bf16[96,128]{1,0:T(8,128)(2,1)S(1)}, bf16[32,128]{1,0:T(8,128)(2,1)S(1)}) custom-call(bf16[96,512]{1,0:T(8,128)(2,1)} %q_hbm.1, bf16[96,128]{1,0:T(8,128)(2,1)} %kv_hbm.1, bf16[32,128]{1,0:T(8,128)(2,1)} %pkv_hbm.1, bf16[96,512]{1,0:T(8,128)(2,1)} %do_hbm.1, s32[16]{0:T(128)} %len_ref.1), custom_call_target="tpu_custom_call" | custom-call | tf_op jit(solution)/shard_map/pallas_call | solution.py:438
  43.1 0.7 %shard_map.85 = (bf16[96,512]{1,0:T(8,128)(2,1)}, bf16[96,512]{1,0:T(8,128)(2,1)}, bf16[96,128]{1,0:T(8,128)(2,1)}, bf16[32,128]{1,0:T(8,128)(2,1)}) custom-call(bf16[96,512]{1,0:T(8,128)(2,1)S(1)} %get-tuple-element.8.refs_0_, bf16[96,512]{1,0:T(8,128)(2,1)S(1)} %get-tuple-element.9.refs_1_, bf16[96,128]{1,0:T(8,128)(2,1)S(1)} %get-tuple-element.10.refs_2_, ...), custom_call_target="tpu_custom_call" | custom-call | tf_op jit(solution)/shard_map/pallas_call | solution.py:472

commit v4 on v3

--- a/solution.py
+++ b/solution.py
@@ -95,6 +95,8 @@
         return pl.ds(pl.multiple_of(GROUP * size_a + py * size_b, size_b), size_b)
 
     def block(off):
+        if not isinstance(off, int):
+            return pl.ds(pl.multiple_of(tail + (reach - 1 - off) * rows, math.gcd(tail, rows)), rows)
         if off == reach:
             return pl.ds(0, tail)
         return pl.ds(tail + (reach - 1 - off) * rows, rows)
@@ -170,7 +172,7 @@
 
     stats = [None, None, None]
 
-    def forward(index, sources, off=None):
+    def forward(slots, sources):
         keys = jnp.concatenate([buffer[0, at_rows] for buffer, at_rows, _, _ in sources], axis=0)
         values = jnp.concatenate([buffer[1, at_rows] for buffer, at_rows, _, _ in sources], axis=0)
         s = dot(keys, qs[...], 1, 1) * to_log2
@@ -194,17 +196,19 @@
             weighted = weighted + stats[2] * shrink
         stats[0], stats[1], stats[2] = high, total, weighted
         done = 0
-        for _, _, base, _ in sources:
+        for slot, (_, _, base, _) in zip(slots, sources):
+            mbuf[slot] = jnp.broadcast_to(high, (8, cols))
             ebuf[base, :] = e[done : done + base.size]
             dpbuf[base, :] = dp[done : done + base.size]
             done += base.size
-        mbuf[index] = jnp.broadcast_to(high, (8, cols))
 
     total_p = count * plocal
 
     def e_block(off):
         rows_at = block(off)
-        return pl.ds(total_p + rows_at.start, rows_at.size)
+        if isinstance(off, int):
+            return pl.ds(total_p + rows_at.start, rows_at.size)
+        return pl.ds(pl.multiple_of(total_p + rows_at.start, math.gcd(tail, rows)), rows)
 
     def index_a(bz):
         return lax.rem(z + bz, GROUP)
@@ -220,6 +224,12 @@
             return kvp, part_b(index_b(n)), part_b(index_b(n)), None
         return kvw, block(n), e_block(n), n
 
+    def slot(item):
+        what, n = item
+        if what == "a":
+            return index_a(n)
+        return GROUP + index_b(n) if what == "b" else GROUP + ny + n
+
     def passed(item):
         what, n = item
         if what == "a":
@@ -232,7 +242,7 @@
         for item in groups[index]:
             buffer, at_rows, _, _ = source(item)
             wait_bytes(buffer.at[other, at_rows], passed(item))
-        forward(index, [source(item) for item in groups[index]])
+        forward([slot(item) for item in groups[index]], [source(item) for item in groups[index]])
 
     def pass_a(bz):
         pz = index_a(bz)
@@ -301,17 +311,20 @@
     inverse = 1.0 / total
     delta = weighted * inverse
 
-    def backward(index):
-        sources = [source(item) for item in groups[index]]
-        factor = jnp.exp2(mbuf[index][:1] - high) * inverse
-        w = jnp.concatenate([ebuf[base, :] for _, _, base, _ in sources], axis=0) * factor
+    def backward(items):
+        sources = [source(item) for item in items]
+        scaled = []
+        for item, (_, _, base, _) in zip(items, sources):
+            factor = jnp.exp2(mbuf[slot(item)][:1] - high) * inverse
+            scaled.append(ebuf[base, :] * factor)
+        w = jnp.concatenate(scaled, axis=0)
         dp = jnp.concatenate([dpbuf[base, :] for _, _, base, _ in sources], axis=0)
         wb = w.astype(BF16)
         ds = (w * (dp - delta)).astype(BF16)
         dk = (dot(ds, qs[...], 1, 0) * scale).astype(BF16)
         dv = dot(wb, dos[...], 1, 0).astype(BF16)
         done = 0
-        for item, (buffer, at_rows, base, _) in zip(groups[index], sources):
+        for item, (buffer, at_rows, base, _) in zip(items, sources):
             now = slice(done, done + base.size)
             done += base.size
             wbuf[base, :] = wb[now]
@@ -327,34 +340,38 @@
             return gw, gwin, gwx_send, gwx_recv.at[n]
         return gp, gpin, gx_send, gx_recv.at[index_a(n) if what == "a" else GROUP + index_b(n)]
 
-    def finish_prompt(index, rows_at, pieces, holds_own):
-        wait_bytes(gpin.at[rows_at], gx_recv.at[index])
-        gpout[rows_at, :] = (gp[kind, rows_at].astype(F32) + gpin[rows_at, :].astype(F32)).astype(BF16)
-        for j, to in pieces:
-            src = gpout.at[pl.ds(pl.multiple_of(rows_at.start + j * plocal, plocal), plocal)]
-            if not holds_own:
-                copy_to(src, rs.at[me], rs_send, rs_recv, {"resp": to})
-                continue
-
-            @pl.when(to != me)
-            def _():
-                copy_to(src, rs.at[me], rs_send, rs_recv, {"resp": to})
+    def both_cores(rows_at, arrived):
+        wait_bytes(gpin.at[rows_at], arrived)
+        total = gp[kind, rows_at].astype(F32) + gpin[rows_at, :].astype(F32)
+        gpout[rows_at, :] = total.astype(BF16)
+
+    def send_piece(index, to):
+        @pl.when(to != me)
+        def _():
+            copy_to(gpout.at[at(index, plocal)], rs.at[me], rs_send, rs_recv, {"resp": to})
 
     def finish_a(bz):
         pz = index_a(bz)
-        turn = [lax.rem(y // 2 + j, ny // 2) for j in range(ny // 2)]
-        pieces = [(j, (2 * j + lax.rem(pz, 2)) * GROUP + pz) for j in turn]
-        finish_prompt(pz, part_a(pz), pieces, bz == 0)
+        both_cores(part_a(pz), gx_recv.at[pz])
+        for j in range(ny // 2):
+            place = lax.rem(y // 2 + j, ny // 2)
+            send_piece(pz * (ny // 2) + place, (2 * place + lax.rem(pz, 2)) * GROUP + pz)
+
+    def send_b(by, place):
+        py = index_b(by)
+        to = py * GROUP + 2 * place + 1 - lax.rem(py, 2)
+        send_piece(GROUP * (ny // 2) + py * (GROUP // 2) + place, to)
 
     def finish_b(by):
         py = index_b(by)
-        pieces = [(j, py * GROUP + 2 * j + 1 - lax.rem(py, 2)) for j in range(GROUP // 2)]
-        finish_prompt(GROUP + py, part_b(py), pieces, by == 0)
+        both_cores(part_b(py), gx_recv.at[GROUP + py])
+        send_b(by, 0)
+        send_b(by, 1)
 
     def finish_window(off):
         wait_bytes(gwin.at[block(off)], gwx_recv.at[off])
         both = gw[kind, block(off)].astype(F32) + gwin[block(off), :].astype(F32)
-        if off == 0:
+        if isinstance(off, int) and off == 0:
             return both
         gwout[block(off), :] = both.astype(BF16)
         size = block(off).size
@@ -365,13 +382,40 @@
         return None
 
     finishes = {"a": finish_a, "b": finish_b, "w": finish_window}
-    back = list(range(len(groups) - 1, -1, -1))
+
+    def ring(r):
+        return ("a", lax.rem(r - z + GROUP, GROUP))
+
+    def columns(parity):
+        return [
+            ("b", lax.rem(2 * lax.rem(y // 2 + j, ny // 2) + parity - y + ny, ny))
+            for j in range(ny // 2)
+        ]
+
+    def nearest(r):
+        return ("w", lax.rem(z - r + GROUP - 1, GROUP) + 1)
+
+    def in_pairs(items):
+        return [items[i : i + 2] for i in range(0, len(items), 2)]
+
+    def send_rest(parity):
+        for _, by in columns(parity):
+            send_b(by, 1)
+
+    far = [("w", off) for off in range(GROUP + 1, reach + 1)]
+    back = [[nearest(0)] + far, [nearest(1)], [("a", 2)]]
+    spread = in_pairs([("b", by) for by in y_order[::-1]])
+    back += spread[:2] + [[("a", 1)], [nearest(2)], [("a", 3)]] + spread[2:]
+    rest = {}
+    back += [[nearest(3)], [("b", 0), ("a", 0)], [("w", 0)]]
     for i in range(len(back) + BEHIND):
         if i < len(back):
             backward(back[i])
         if i >= BEHIND:
-            for what, n in groups[back[i - BEHIND]]:
+            for what, n in back[i - BEHIND]:
                 own_grad = finishes[what](n)
+            if i - BEHIND in rest:
+                send_rest(rest[i - BEHIND])
     rs[me] = gpout[own_p, :]
 
     p_part = pl.ds(0, total_p)

time: 43.9 us -> 42.6 us (0.970)
  Pallas kernels: 43.1 us -> 41.8 us
    pallas_call x1, Pallas kernels: 42.4 us -> 41.1 us  [shards(): pl.pallas_call(functools.partial(kernel, count), out_shape=tuple((pltpu.V...]
where the time goes in v4:
time: 42.6 us; the launch traced here: 42.4 us
  Pallas kernels  41.8 us (98%)
  between operations  0.64 us (2%)
    pallas_call x1, Pallas kernels, shards(): pl.pallas_call(functools.partial(kernel, count), out_shape=tuple((pltpu.V...  41.1 us

profile of v4, /device:TPU:1, one launch (start us, length us, event | category | flops | bytes accessed | tf_op | source)
XLA Modules:
  0.0 42.4 jit_solution(17518990768042353731)
XLA Ops:
  0.6 41.1 %shard_map.84 = (bf16[96,512]{1,0:T(8,128)(2,1)S(1)}, bf16[96,512]{1,0:T(8,128)(2,1)S(1)}, bf16[96,128]{1,0:T(8,128)(2,1)S(1)}, bf16[32,128]{1,0:T(8,128)(2,1)S(1)}) custom-call(bf16[96,512]{1,0:T(8,128)(2,1)} %q_hbm.1, bf16[96,128]{1,0:T(8,128)(2,1)} %kv_hbm.1, bf16[32,128]{1,0:T(8,128)(2,1)} %pkv_hbm.1, bf16[96,512]{1,0:T(8,128)(2,1)} %do_hbm.1, s32[16]{0:T(128)} %len_ref.1), custom_call_target="tpu_custom_call" | custom-call | tf_op jit(solution)/shard_map/pallas_call | solution.py:482
  41.7 0.7 %shard_map.85 = (bf16[96,512]{1,0:T(8,128)(2,1)}, bf16[96,512]{1,0:T(8,128)(2,1)}, bf16[96,128]{1,0:T(8,128)(2,1)}, bf16[32,128]{1,0:T(8,128)(2,1)}) custom-call(bf16[96,512]{1,0:T(8,128)(2,1)S(1)} %get-tuple-element.8.refs_0_, bf16[96,512]{1,0:T(8,128)(2,1)S(1)} %get-tuple-element.9.refs_1_, bf16[96,128]{1,0:T(8,128)(2,1)S(1)} %get-tuple-element.10.refs_2_, ...), custom_call_target="tpu_custom_call" | custom-call | tf_op jit(solution)/shard_map/pallas_call | solution.py:516
